TPU v7x, 256 devices: a whole 4x4x8 slice. The times are simulated.
256 devices in a mesh: clip: 16 (over y, z_lo, core), text: 16 (over x, z_hi).
Axes of the slice: x: 4, y: 4, z: 8 (z_hi: 4, z_lo: 2; z = z_hi * 2 + z_lo), core: 2. Of those that a mesh axis runs over, the one named last changes fastest.
Arguments:
- clip_emb: bfloat16 [16384, 1152], P(('clip', 'text')), may hold values from -0.19921875 to 0.19921875
- text_emb: bfloat16 [16, 1024, 1152], P('text', 'clip'), may hold values from -0.19921875 to 0.19921875
- positive: int32 [16384], P('clip'), may hold values from 0 to 16383, each once
- log_temp: float32 [], replicated, may hold values from 2.3 to 3
- bias: float32 [], replicated, may hold values from -7 to -5
Outputs:
- loss: float32 [], replicated
- grad_clip: float32 [16384, 1152], P(('clip', 'text'))
- grad_text: float32 [16, 1024, 1152], P('text', 'clip')
- grad_temp: float32 [], replicated
- grad_bias: float32 [], replicated
All inputs are finite; a program needn't handle non-finite values.
Results may differ from a plain program's by a relative error of at most 0.0044.
Values may be sent and summed in bfloat16 or wider, within the bound.
A program may use at most 64 MiB of HBM per device.

v0:
```python
import jax
import jax.numpy as jnp
from jax import lax
from jax.sharding import PartitionSpec as P


def unit_rows(emb):
    wide = emb.astype(jnp.float32)
    scale = lax.rsqrt(jnp.sum(wide * wide, axis=1, keepdims=True) + 1e-06)
    normal = wide * scale
    return (scale, normal, normal.astype(jnp.bfloat16))


def per_device(clip_emb, text_emb, positive, log_temp, bias):
    clip_full = lax.all_gather(clip_emb, "text", axis=0, tiled=True)
    text_full = lax.all_gather(text_emb, "clip", axis=1, tiled=True)[0]
    clip_scale, clip_norm, clip_unit = unit_rows(clip_full)
    text_scale, text_norm, text_unit = unit_rows(text_full)
    temp = jnp.exp(log_temp)
    clip_rows = clip_full.shape[0]
    text_rows = text_full.shape[0]
    width = clip_full.shape[1]
    pairs = clip_rows * lax.axis_size("clip")
    text_first = lax.axis_index("text") * text_rows
    sims = lax.dot_general(
        clip_unit, text_unit, (((1,), (1,)), ((), ())), preferred_element_type=jnp.float32
    )
    logits = temp * sims + bias
    columns = text_first + jnp.arange(text_rows, dtype=jnp.int32)
    sign = jnp.where(positive[:, None] == columns[None, :], 1.0, -1.0).astype(jnp.float32)
    loss_part = -jnp.sum(jax.nn.log_sigmoid(sign * logits))
    dlogit = -sign * jax.nn.sigmoid(-sign * logits)
    bias_part = jnp.sum(dlogit)
    temp_part = jnp.sum(dlogit * sims)
    loss_sum, bias_sum, temp_sum = lax.psum((loss_part, bias_part, temp_part), ("clip", "text"))
    dlogit_low = dlogit.astype(jnp.bfloat16)
    clip_cols = width // lax.axis_size("text")
    text_cols = width // lax.axis_size("clip")
    clip_part = jnp.dot(dlogit_low, text_unit, preferred_element_type=jnp.float32)
    clip_share = temp * lax.psum_scatter(clip_part, "text", scatter_dimension=1, tiled=True)
    text_part = lax.dot_general(
        dlogit_low, clip_unit, (((0,), (0,)), ((), ())), preferred_element_type=jnp.float32
    )
    text_share = temp * lax.psum_scatter(text_part, "clip", scatter_dimension=1, tiled=True)
    clip_norm_share = lax.dynamic_slice_in_dim(
        clip_norm, lax.axis_index("text") * clip_cols, clip_cols, 1
    )
    text_norm_share = lax.dynamic_slice_in_dim(
        text_norm, lax.axis_index("clip") * text_cols, text_cols, 1
    )
    clip_inner = lax.psum(jnp.sum(clip_norm_share * clip_share, axis=1), "text")
    text_inner = lax.psum(jnp.sum(text_norm_share * text_share, axis=1), "clip")
    clip_done = clip_scale * (clip_share - clip_norm_share * clip_inner[:, None])
    text_done = text_scale * (text_share - text_norm_share * text_inner[:, None])
    grad_clip = lax.all_to_all(clip_done, "text", split_axis=0, concat_axis=1, tiled=True)
    text_mine = lax.all_to_all(text_done, "clip", split_axis=0, concat_axis=1, tiled=True)
    grad_text = text_mine[None, :, :]
    loss = loss_sum / pairs
    grad_temp = temp * temp_sum / pairs
    grad_bias = bias_sum / pairs
    return (loss, grad_clip, grad_text, grad_temp, grad_bias)


def solution(mesh):
    return jax.shard_map(
        per_device,
        mesh=mesh,
        in_specs=(P(("clip", "text"), None), P("text", "clip", None), P("clip"), P(), P()),
        out_specs=(P(), P(("clip", "text"), None), P("text", "clip", None), P(), P()),
        check_vma=False,
    )
```

profile of v0, /device:TPU:1, one launch (start us, length us, event | category | flops | bytes accessed | tf_op | source)
XLA Modules:
  0.0 448.2 jit_solution(14714952923982447142)
XLA Ops:
  7.2 0.0 all-gather.5.cloned.1.call-start
  7.2 0.7 all-gather.5.cloned.1.call-update
  7.9 0.0 all-gather.3.cloned.1.call-start
  7.9 0.7 all-gather.3.cloned.1.call-update
  8.6 0.0 reduce-scatter.5.cloned.1.call-start
  10.0 41.1 %all-gather.5.cloned.1.call-done = bf16[1,1024,1152]{2,1,0:T(8,128)(2,1)} async-done(((bf16[1,64,1152]{2,1,0:T(8,128)(2,1)}), bf16[1,1024,1152]{2,1,0:T(8,128)(2,1)}) %all-gather.5.cloned.1.call-update) | async-done | bytes 2359312 | tf_op jit(solution)/shard_map/all_gather | solution.py:16
  51.1 2.8 copy.21
  53.9 0.0 copy-start
  54.0 0.0 copy-start.1
  54.0 0.5 fusion.3
  54.5 0.8 copy-done
  55.3 58.9 %all-gather.3.cloned.1.call-done = bf16[1024,1152]{1,0:T(8,128)(2,1)} async-done(((bf16[64,1152]{1,0:T(8,128)(2,1)}), bf16[1024,1152]{1,0:T(8,128)(2,1)}) %all-gather.3.cloned.1.call-update) | async-done | bytes 2359312 | tf_op jit(solution)/shard_map/all_gather | solution.py:15
  114.2 2.8 copy.20
  117.1 0.5 fusion.2
  117.6 0.0 copy-done.1
  117.6 9.9 %fusion.19 = (f32[]{:T(128)}, f32[]{:T(128)}, f32[]{:T(128)}, bf16[1024,1024]{1,0:T(8,128)(2,1)S(1)}) fusion(f32[]{:T(128)S(6)} %copy.29, f32[]{:T(128)S(6)} %exp.11, s32[1024]{0:T(1024)S(1)} %iota_add_fusion, s32[1024]{0:T(1024)S(1)} %copy-done.1, f32[1024]{0:T(1024)S(1)} %add_rsqrt_fusion, bf16[1,1024,1152]{1,2,0:T(8,128)(2,1)} %copy-done, ...), kind=kOutput, calls=%fused_computation.35 | convolution fusion | flops 2447114240 | bytes 6832148 | tf_op jit(solution)/shard_map/dot_general | solution.py:25
  127.5 0.0 copy-start.2
  127.5 1.3 copy-done.2
  128.8 4.3 fusion.14
  133.1 0.0 reduce-scatter.5.cloned.1.call-update
  133.2 0.0 reduce-scatter.3.cloned.1.call-start
  133.2 7.1 %fusion.10 = f32[1024,1152]{0,1:T(8,128)} fusion(bf16[1,1024,1152]{1,2,0:T(8,128)(2,1)} %copy-done, f32[1024]{0:T(1024)S(1)} %add_rsqrt_fusion, bf16[1024,1024]{1,0:T(8,128)(2,1)} %copy-done.2), kind=kOutput, calls=%fused_computation.19 | convolution fusion | flops 2419458048 | bytes 9179136 | tf_op jit(solution)/shard_map/dot_general | solution.py:39
  140.3 0.0 reduce-scatter.3.cloned.1.call-update
  140.3 4.6 %convert_multiply_fusion = f32[1024,1152]{0,1:T(8,128)} fusion(bf16[1,1024,1152]{1,2,0:T(8,128)(2,1)} %copy-done, f32[1024]{0:T(1024)S(1)} %add_rsqrt_fusion), kind=kLoop, calls=%fused_computation.1 | loop fusion | flops 2359296 | bytes 7081984 | tf_op jit(solution)/shard_map/mul | solution.py:10
  144.9 57.9 %reduce-scatter.5.cloned.1.call-done = f32[1024,72]{0,1:T(8,128)} async-done(((f32[1024,1152]{0,1:T(8,128)}), f32[1024,72]{0,1:T(8,128)}) %reduce-scatter.5.cloned.1.call-update) | async-done | bytes 294928 | tf_op jit(solution)/shard_map/reduce_scatter | solution.py:44
  202.8 1.1 multiply_reduce_fusion.1
  203.9 30.0 %psum.37 = f32[1024]{0:T(1024)S(1)} all-reduce(f32[1024]{0:T(1024)S(1)} %multiply_reduce_fusion.1), channel_id=1, replica_groups=mesh['clip'=16,'text'=16] {'clip'}, use_global_device_ids=true, to_apply=%region_9.10 | all-reduce | flops 1024 | bytes 8192 | tf_op jit(solution)/shard_map/psum | solution.py:52
  233.8 1.1 subtract_multiply_fusion
  234.9 1.0 copy.27
  235.9 6.2 %all-to-all-start.1 = ((f32[16,64,72]{2,1,0:T(8,128)}), f32[16,64,72]{2,1,0:T(8,128)S(1)}, u32[]{:S(2)}, u32[]{:S(2)}) async-start(f32[16,64,72]{2,1,0:T(8,128)} %bitcast.4), calls=%async_computation.3 | async-start | bytes 1048576 | tf_op jit(solution)/shard_map/all_to_all | solution.py:56
  242.2 2.8 convert_multiply_fusion.2
  245.0 61.6 %reduce-scatter.3.cloned.1.call-done = f32[1024,72]{0,1:T(8,128)} async-done(((f32[1024,1152]{0,1:T(8,128)}), f32[1024,72]{0,1:T(8,128)}) %reduce-scatter.3.cloned.1.call-update) | async-done | bytes 294928 | tf_op jit(solution)/shard_map/reduce_scatter | solution.py:40
  306.6 1.1 multiply_reduce_fusion.2
  307.7 35.2 %psum.36 = f32[1024]{0:T(1024)S(1)} all-reduce(f32[1024]{0:T(1024)S(1)} %multiply_reduce_fusion.2), channel_id=1, replica_groups=mesh['clip'=16,'text'=16] {'text'}, use_global_device_ids=true, to_apply=%region_6.7 | all-reduce | flops 1024 | bytes 8192 | tf_op jit(solution)/shard_map/psum | solution.py:51
  342.9 1.1 subtract_multiply_fusion.1
  344.0 1.0 copy.26
  345.0 0.0 all-to-all-done.1
  345.0 3.6 all-to-all-start
  348.6 85.1 %all-reduce = (f32[]{:T(128)}, f32[]{:T(128)}, f32[]{:T(128)}) all-reduce(f32[]{:T(128)} %get-tuple-element.7, f32[]{:T(128)} %get-tuple-element.6, f32[]{:T(128)} %get-tuple-element.5), channel_id=1, replica_groups=mesh['clip'=16,'text'=16] {'clip','text'}, use_global_device_ids=true, to_apply=%region_3.4 | all-reduce | flops 3 | bytes 24 | tf_op jit(solution)/shard_map/psum | solution.py:35
  435.7 0.3 copy.25
  436.0 1.0 broadcast_in_dim.19
  437.0 0.0 all-to-all-done
  437.0 0.3 copy.23
  437.3 1.0 all_to_all.29
  (3 shorter events, 0.0 us)
Async XLA Ops:
  7.2 43.9 %all-gather.5.cloned.1.call-start = ((), (), s32[]{:S(2)}) async-start(), calls=%async_computation.5 | async-start | bytes 2506752 | tf_op jit(solution)/shard_map/all_gather | solution.py:16
  7.9 106.3 %all-gather.3.cloned.1.call-start = ((), (), s32[]{:S(2)}) async-start(), calls=%async_computation.4 | async-start | bytes 2506752 | tf_op jit(solution)/shard_map/all_gather | solution.py:15
  8.6 194.1 %reduce-scatter.5.cloned.1.call-start = ((), (), s32[]{:S(2)}) async-start(), calls=%async_computation.7 | async-start | bytes 5013504 | tf_op jit(solution)/shard_map/reduce_scatter | solution.py:44
  53.9 1.4 copy-start
  54.0 63.7 %copy-start.1 = (s32[1024]{0:T(1024)S(1)}, s32[1024]{0:T(1024)}, u32[]{:S(2)}) copy-start(s32[1024]{0:T(1024)} %param.7) | copy-start | bytes 12292
  127.5 1.3 copy-start.2
  133.2 173.5 %reduce-scatter.3.cloned.1.call-start = ((), (), s32[]{:S(2)}) async-start(), calls=%async_computation.6 | async-start | bytes 5013504 | tf_op jit(solution)/shard_map/reduce_scatter | solution.py:40
  235.9 109.1 %all-to-all-start.1 = ((f32[16,64,72]{2,1,0:T(8,128)}), f32[16,64,72]{2,1,0:T(8,128)S(1)}, u32[]{:S(2)}, u32[]{:S(2)}) async-start(f32[16,64,72]{2,1,0:T(8,128)} %bitcast.4), calls=%async_computation.3 | async-start | bytes 1048576 | tf_op jit(solution)/shard_map/all_to_all | solution.py:56
  345.0 91.9 %all-to-all-start = ((f32[16,64,72]{2,1,0:T(8,128)}), f32[16,64,72]{2,1,0:T(8,128)S(1)}, u32[]{:S(2)}, u32[]{:S(2)}) async-start(f32[16,64,72]{2,1,0:T(8,128)} %bitcast.2), calls=%async_computation.1 | async-start | bytes 1048576 | tf_op jit(solution)/shard_map/all_to_all | solution.py:55
Sparse Core Ops, SparseCore 0:
  9.8 41.2 all-gather.4
  53.6 60.6 all-gather.2
  133.3 69.4 reduce-scatter.4
  206.3 100.3 reduce-scatter.2
where the time goes:
time: 449 us; the launch traced here: 448 us
  waiting for transfers between devices  221 us (49%)
  blocking collectives  150 us (33%)
  matrix products  21.3 us (5%)
  between operations  20.5 us (5%)
  other arithmetic  12.9 us (3%)
  local copies, waits for them, and re-layouts  12.3 us (3%)
  starting transfers between devices  9.95 us (2%)
    psum x1, blocking collectives, per_device(): lax.psum((loss_part, bias_part, temp_part), ('clip', 'text'))  85.1 us
    reduce_scatter x1, waiting for transfers between devices, per_device(): lax.psum_scatter(clip_part, 'text', scatter_dimension=1, tiled=True)  61.6 us
    all_gather x1, waiting for transfers between devices, per_device(): clip_full = lax.all_gather(clip_emb, 'text', axis=0, tiled=True)  58.9 us
    reduce_scatter x1, waiting for transfers between devices, per_device(): lax.psum_scatter(text_part, 'clip', scatter_dimension=1, tiled=True)  57.9 us
    all_gather x1, waiting for transfers between devices, per_device(): text_full = lax.all_gather(text_emb, 'clip', axis=1, tiled=True)[0]  41.1 us
    psum x1, blocking collectives, per_device(): clip_inner = lax.psum(jnp.sum(clip_norm_share * clip_share, axis=1), 'text')  35.2 us
    psum x1, blocking collectives, per_device(): text_inner = lax.psum(jnp.sum(text_norm_share * text_share, axis=1), 'clip')  30 us
    dot_general x1, matrix products, per_device(): lax.dot_general(clip_unit, text_unit, (((1,), (1,)), ((), ())), preferred...  9.87 us
  transfers between devices with their start and end apart: 6, of which 4 were waited for; matrix products, arithmetic and copies ran while one was open for 6% of the time, Pallas kernels for 0%

commit v1 on v0

v1 whole, which is shorter than its diff:
```python
import jax
import jax.numpy as jnp
from jax import lax
from jax.experimental import pallas as pl
from jax.experimental.pallas import tpu as pltpu
from jax.sharding import PartitionSpec as P

MESH = pl.DeviceIdType.MESH
F32 = jnp.float32
BF16 = jnp.bfloat16
LOG2E = 1.4426950408889634
D = 1152
ROWS = 64
HALF = 32
TILE = 1024

CLIP_BLOCK = {0: 0, 1: 1, 3: 2, 2: 3}
TEXT_GROUP = {4: 0, 0: 1, 3: 2, 5: 3, 2: 4, 6: 5, 1: 6, 7: 7}


def clip_at(half, apart, index):
    return CLIP_BLOCK[apart] * 256 + half * 128 + index * HALF


def text_at(dz, dk):
    return TEXT_GROUP[dz] * 128 + dk * ROWS


def kernel(
    clip_ref, text_ref, pos_ref, log_temp_ref, bias_ref,
    grad_clip_ref, grad_text_ref, loss_ref, grad_temp_ref, grad_bias_ref,
    clu, txu, posb, posc, colid, dl, gc, gt, acc,
    cs1, cr1, cs2, cr2, cs3, cr3, ks, kr, zs, zr, sums, sumr,
    clip_send, clip_recv, text_send, text_recv, core_send, core_recv, pos_send, pos_recv,
    c1_send, c1_recv, c2_send, c2_recv, c3_send, c3_recv, k_send, k_recv, z_send, z_recv, s_send, s_recv,
):
    c = lax.axis_index("clip")
    t = lax.axis_index("text")
    x, y, z, k = t // 4, c // 4, (t % 4) * 2 + (c // 2) % 2, c % 2

    def dev(dx=0, dy=0, dz=0, dk=0):
        ax, ay, az, ak = (x + dx) % 4, (y + dy) % 4, (z + dz) % 8, (k + dk) % 2
        return (ay * 4 + (az % 2) * 2 + ak, ax * 4 + az // 2)

    def along(half, step):
        return dev(dy=step) if half == 0 else dev(dx=step)

    def across(half, step):
        return dev(dx=step) if half == 0 else dev(dy=step)

    started = []

    def send(src, dst, ssem, rsem, to):
        copy = pltpu.make_async_remote_copy(
            src_ref=src, dst_ref=dst, send_sem=ssem, recv_sem=rsem, device_id=to, device_id_type=MESH
        )
        copy.start()
        started.append(copy)
        return copy

    peers = [dev(dx=i) for i in (1, 2, 3)] + [dev(dy=i) for i in (1, 2, 3)]
    peers += [dev(dz=i) for i in range(1, 8)] + [dev(dk=1)]
    barrier = pltpu.get_barrier_semaphore()
    for peer in peers:
        pl.semaphore_signal(barrier, inc=1, device_id=peer, device_id_type=MESH)

    def unit_rows(ref):
        wide = ref[...].astype(F32)
        scale = lax.rsqrt(jnp.sum(wide * wide, axis=1, keepdims=True) + 1e-06)
        return scale, wide * scale

    clip_unit = unit_rows(clip_ref)[1].astype(BF16)
    for half in (0, 1):
        clu[pl.ds(clip_at(half, 0, 0), HALF), :] = clip_unit[half * HALF:(half + 1) * HALF, :]
    txu[pl.ds(text_at(0, 0), ROWS), :] = unit_rows(text_ref)[1].astype(BF16)
    posb[0] = pos_ref[...]

    pl.semaphore_wait(barrier, len(peers))

    def text_piece(dz, dk, half):
        return txu.at[pl.ds(text_at(dz, dk) + half * HALF, HALF)]

    text_copy = {}

    def text_hop(src_dz, step, half):
        dst_dz = (src_dz - step) % 8
        text_copy[dst_dz, half] = send(
            text_piece(src_dz, 0, half), text_piece(dst_dz, 0, half),
            text_send.at[dst_dz, half], text_recv.at[dst_dz, half], dev(dz=step),
        )

    core_copy = {}

    def text_core(dz):
        rows = pl.ds(text_at(dz, 0), ROWS)
        core_copy[dz] = send(
            txu.at[rows], txu.at[pl.ds(text_at(dz, 1), ROWS)], core_send.at[dz], core_recv.at[dz], dev(dk=1)
        )

    clip_copy = {}

    def clip_piece(half, apart, index):
        return clu.at[pl.ds(clip_at(half, apart, index), HALF)]

    def clip_first(half, step):
        index = (-step) % 4
        clip_copy[half, 0, index] = send(
            clip_piece(half, 0, 0), clip_piece(half, 0, index),
            clip_send.at[half, 0, index], clip_recv.at[half, 0, index], across(half, step),
        )

    def clip_second(half, src_apart, index, step):
        apart = (src_apart - step) % 4
        clip_copy[half, apart, index] = send(
            clip_piece(half, src_apart, index), clip_piece(half, apart, index),
            clip_send.at[half, apart, index], clip_recv.at[half, apart, index], along(half, step),
        )

    for step in (1, -1, 2):
        for half in (0, 1):
            clip_first(half, step)
    for half in (0, 1):
        text_hop(0, 1, half)
        text_hop(0, -1, 1 - half)
    for half in (0, 1):
        clip_second(half, 0, 0, 1)
        clip_second(half, 0, 0, -1)
    text_core(0)
    pos_copy = [
        send(posb.at[0], posb.at[(-step) % 4], pos_send.at[step], pos_recv.at[step], dev(dy=step)) for step in (1, 2, 3)
    ]

    lane = lax.broadcasted_iota(jnp.int32, (8, 128), 1)
    for dz in range(8):
        az = (z + dz) % 8
        base = (x * 4 + az // 2) * 1024 + (y * 4 + (az % 2) * 2) * ROWS
        ids = jnp.where(lane < ROWS, base + k * ROWS, base + (1 - k) * ROWS) + lane % ROWS
        colid[:, pl.ds(text_at(dz, 0), 128)] = ids.astype(F32)

    order = {0: (1, 3, 2), 1: (1, 3, 2)}
    for index in order[0]:
        for half in (0, 1):
            clip_copy[half, 0, index].wait_recv()
            clip_second(half, 0, index, 1 if index < 2 else -1)
            clip_second(half, 0, index, -1 if index < 2 else 1)
    for dz, step in ((7, 1), (1, -1)):
        for half in (0, 1) if step == 1 else (1, 0):
            text_copy[dz, half].wait_recv()
            text_hop(dz, step, half)
        text_core(dz)
    for half in (0, 1):
        for index in (0, 1):
            clip_copy[half, 3, index].wait_recv()
            clip_second(half, 3, index, 1)
        for index in (3, 2):
            clip_copy[half, 1, index].wait_recv()
            clip_second(half, 1, index, -1)
    for dz, step in ((6, 1), (2, -1)):
        for half in (0, 1) if step == 1 else (1, 0):
            text_copy[dz, half].wait_recv()
            text_hop(dz, step, half)
        text_core(dz)

    for copy in pos_copy:
        copy.wait_recv()
    z_hi = z // 2
    row_in = lax.broadcasted_iota(jnp.int32, (HALF, 128), 0)
    lane_in = lax.broadcasted_iota(jnp.int32, (HALF, 128), 1)
    for half in (0, 1):
        hit = lane_in == row_in + ((z_hi % 2) * ROWS + half * HALF)
        for dx in range(4):
            for dy in range(4):
                apart, index = (dy, dx) if half == 0 else (dx, dy)
                row = ((x + dx) % 4) * 2 + z_hi // 2
                values = posb[dy, pl.ds(row, 1), :].astype(F32)
                posc[pl.ds(clip_at(half, apart, index), HALF), :] = jnp.sum(
                    jnp.where(hit, values, 0.0), axis=1, keepdims=True
                )

    for dz, step in ((5, 1), (3, -1)):
        for half in (0, 1) if step == 1 else (1, 0):
            text_copy[dz, half].wait_recv()
            if half == (0 if step == 1 else 1):
                text_hop(dz, step, half)
        text_core(dz)
    for half in (0, 1):
        text_copy[4, half].wait_recv()
    text_core(4)
    for half in (0, 1):
        for index in (2, 3):
            clip_copy[half, 3, index].wait_recv()
        for index in (0, 1):
            clip_copy[half, 1, index].wait_recv()
        for index in range(4):
            clip_copy[half, 2, index].wait_recv()
    for dz in range(8):
        core_copy[dz].wait_recv()

    temp = jnp.exp(jnp.full((8, 128), log_temp_ref[0, 0], F32))
    factor = (temp * LOG2E)[0:1, 0:1]
    offset = bias_ref[0, 0] * LOG2E
    acc[...] = jnp.zeros_like(acc)

    def fold(value):
        return jnp.sum(value.reshape(32, 8, 8, 128), axis=(0, 2))

    def block(i, carry):
        rows = pl.ds(pl.multiple_of(i * 256, 256), 256)
        sims = lax.dot_general(clu[rows, :], txu[...], (((1,), (1,)), ((), ())), preferred_element_type=F32)
        e = jnp.exp2(sims * factor + offset)
        plus = 1.0 + e
        inverse = 1.0 / plus
        mask = posc[rows, :] == colid[0:1, :]
        dlogit = jnp.where(mask, -inverse, e * inverse)
        acc[0] += fold(jnp.log(plus))
        acc[1] += fold(dlogit)
        acc[2] += fold(dlogit * sims)
        acc[3] += fold(jnp.where(mask, sims, 0.0))
        dl[rows, :] = dlogit.astype(BF16)
        return carry

    lax.fori_loop(0, 4, block, 0)

    sum_copy = []

    def share(slots, targets):
        copies = [
            send(sums.at[slots[0]], sumr.at[slot], s_send.at[slot], s_recv.at[slot], to)
            for slot, to in zip(slots, targets)
        ]
        return copies

    def collect(copies, slots, nxt):
        total = sums[slots[0]]
        for copy, slot in zip(copies, slots):
            copy.wait_recv()
            total = total + sumr[slot]
        sums[nxt] = total

    for i in range(4):
        sums[0, pl.ds(i, 1), :] = jnp.sum(acc[i], axis=0, keepdims=True)
    sums[0, pl.ds(4, 4), :] = jnp.zeros((4, 128), F32)
    core_slots, x_slots, y_slots, z_slots = (0,), (1, 2, 3), (4, 5, 6), tuple(range(7, 14))
    core_share = share(core_slots, [dev(dk=1)])

    def text_grad(i):
        rows = pl.ds(i * 256, 256)
        gt[rows, :] = lax.dot_general(dl[:, i * 256:(i + 1) * 256], clu[...], (((0,), (0,)), ((), ())), preferred_element_type=F32)

    def clip_grad(i):
        rows = pl.ds(i * 256, 256)
        gc[rows, :] = lax.dot_general(dl[rows, :], txu[...], (((1,), (0,)), ((), ())), preferred_element_type=F32)

    k_copy = {}

    def to_core(dz):
        ks[dz] = gt[pl.ds(text_at(dz, 1), ROWS), :].astype(BF16)
        k_copy[dz] = send(ks.at[dz], kr.at[dz], k_send.at[dz], k_recv.at[dz], dev(dk=1))

    def text_sum(dz, half):
        return gt[pl.ds(text_at(dz, 0) + half * HALF, HALF), :] + kr[dz, pl.ds(half * HALF, HALF), :].astype(F32)

    z_copy = {}

    def ring(way, stage, half, dz):
        part = pl.ds(half * HALF, HALF)
        value = text_sum(dz, half)
        if (way, stage - 1, half) in z_copy:
            z_copy[way, stage - 1, half].wait_recv()
            value = value + zr[way, stage - 1, part, :].astype(F32)
        zs[dz, part, :] = value.astype(BF16)
        z_copy[way, stage, half] = send(
            zs.at[dz, part], zr.at[way, stage, part], z_send.at[way, stage, half], z_recv.at[way, stage, half],
            dev(dz=1 if way == 0 else -1),
        )

    c1_copy = {}
    c2_copy = {}
    c3_copy = {}

    def clip_r1(half):
        for index in range(4):
            cs1[half, index] = gc[pl.ds(clip_at(half, 2, index), HALF), :].astype(BF16)
            c1_copy[half, index] = send(
                cs1.at[half, index], cr1.at[half, index], c1_send.at[half, index], c1_recv.at[half, index],
                along(half, 1 if index < 2 else -1),
            )

    def clip_r2(half, way):
        apart = 1 if way == 0 else 3
        passed = (0, 1) if way == 0 else (2, 3)
        for index in (2, 3, 0, 1) if way == 0 else (0, 1, 2, 3):
            value = gc[pl.ds(clip_at(half, apart, index), HALF), :]
            if index in passed:
                c1_copy[half, index].wait_recv()
                value = value + cr1[half, index].astype(F32)
            cs2[half, way, index] = value.astype(BF16)
            c2_copy[half, way, index] = send(
                cs2.at[half, way, index], cr2.at[half, way, index],
                c2_send.at[half, way, index], c2_recv.at[half, way, index],
                along(half, 1 if way == 0 else -1),
            )

    def clip_r3(half):
        for index in (2, 1, 3, 0):
            value = gc[pl.ds(clip_at(half, 0, index), HALF), :]
            for way in (0, 1):
                c2_copy[half, way, index].wait_recv()
                value = value + cr2[half, way, index].astype(F32)
            if index == 0:
                gc[pl.ds(clip_at(half, 0, 0), HALF), :] = value
            else:
                cs3[half, index - 1] = value.astype(BF16)
                c3_copy[half, index] = send(
                    cs3.at[half, index - 1], cr3.at[half, index - 1],
                    c3_send.at[half, index - 1], c3_recv.at[half, index - 1], across(half, index),
                )

    text_grad(0)
    to_core(4)
    text_grad(1)
    to_core(3)
    to_core(5)
    clip_grad(3)
    clip_r1(0)
    clip_r1(1)
    collect(core_share, core_slots, 1)
    x_share = share(x_slots, [dev(dx=i) for i in (1, 2, 3)])
    k_copy[4].wait_recv()
    ring(0, 0, 0, 4)
    ring(1, 0, 1, 4)
    text_grad(2)
    to_core(2)
    to_core(6)
    k_copy[3].wait_recv()
    k_copy[5].wait_recv()
    ring(0, 1, 1, 3)
    ring(1, 1, 0, 5)
    clip_grad(1)
    clip_grad(2)
    for half in (0, 1):
        clip_r2(half, 0)
        clip_r2(half, 1)
    ring(0, 1, 0, 3)
    ring(1, 1, 1, 5)
    text_grad(3)
    to_core(1)
    to_core(7)
    to_core(0)
    k_copy[2].wait_recv()
    k_copy[6].wait_recv()
    collect(x_share, x_slots, 4)
    y_share = share(y_slots, [dev(dy=i) for i in (1, 2, 3)])
    clip_grad(0)
    for half in (1, 0):
        ring(0, 2, half, 2)
        ring(1, 2, 1 - half, 6)
    for half in (0, 1):
        clip_r3(half)
    collect(y_share, y_slots, 7)
    z_share = share(z_slots, [dev(dz=i) for i in range(1, 8)])
    k_copy[1].wait_recv()
    k_copy[7].wait_recv()
    for half in (1, 0):
        ring(0, 3, half, 1)
        ring(1, 3, 1 - half, 7)

    def finish(scale, normal, back):
        return scale * (back - normal * jnp.sum(normal * back, axis=1, keepdims=True))

    temp_one = temp[0:1, 0:1]
    clip_scale, clip_norm = unit_rows(clip_ref)
    for half in (0, 1):
        value = gc[pl.ds(clip_at(half, 0, 0), HALF), :]
        for index in (1, 2, 3):
            c3_copy[half, index].wait_recv()
            value = value + cr3[half, index - 1].astype(F32)
        part = slice(half * HALF, (half + 1) * HALF)
        grad_clip_ref[part, :] = finish(clip_scale[part], clip_norm[part], temp_one * value)
    k_copy[0].wait_recv()
    text_scale, text_norm = unit_rows(text_ref)
    for half in (0, 1):
        value = text_sum(0, half)
        for way in (0, 1):
            z_copy[way, 3, half].wait_recv()
            value = value + zr[way, 3, pl.ds(half * HALF, HALF), :].astype(F32)
        part = slice(half * HALF, (half + 1) * HALF)
        grad_text_ref[part, :] = finish(text_scale[part], text_norm[part], temp_one * value)

    collect(z_share, z_slots, 14)
    total = sums[14]
    pairs = 16384.0
    log_sum = jnp.sum(total[0:1, :])
    bias_sum = jnp.sum(total[1:2, :])
    temp_sum = jnp.sum(total[2:3, :])
    positive_sum = jnp.sum(total[3:4, :])
    temp_scalar = jnp.sum(jnp.where(lane == 0, temp, 0.0)[0:1, :])
    loss_ref[0, 0] = (log_sum - temp_scalar * positive_sum) / pairs - bias_ref[0, 0]
    grad_temp_ref[0, 0] = temp_scalar * temp_sum / pairs
    grad_bias_ref[0, 0] = bias_sum / pairs

    for copy in started:
        copy.wait_send()


def per_device(clip_emb, text_emb, positive, log_temp, bias):
    vmem = pl.BlockSpec(memory_space=pltpu.VMEM)
    smem = pl.BlockSpec(memory_space=pltpu.SMEM)
    one = jax.ShapeDtypeStruct((1, 1), F32)
    rows = jax.ShapeDtypeStruct((ROWS, D), F32)
    dma = pltpu.SemaphoreType.DMA
    grad_clip, grad_text, loss, grad_temp, grad_bias = pl.pallas_call(
        kernel,
        out_shape=(rows, rows, one, one, one),
        in_specs=[vmem, vmem, vmem, smem, smem],
        out_specs=(vmem, vmem, smem, smem, smem),
        scratch_shapes=[
            pltpu.VMEM((TILE, D), BF16),
            pltpu.VMEM((TILE, D), BF16),
            pltpu.VMEM((4, 8, 128), jnp.int32),
            pltpu.VMEM((TILE, 1), F32),
            pltpu.VMEM((8, TILE), F32),
            pltpu.VMEM((TILE, TILE), BF16),
            pltpu.VMEM((TILE, D), F32),
            pltpu.VMEM((TILE, D), F32),
            pltpu.VMEM((4, 8, 128), F32),
            pltpu.VMEM((2, 4, HALF, D), BF16),
            pltpu.VMEM((2, 4, HALF, D), BF16),
            pltpu.VMEM((2, 2, 4, HALF, D), BF16),
            pltpu.VMEM((2, 2, 4, HALF, D), BF16),
            pltpu.VMEM((2, 3, HALF, D), BF16),
            pltpu.VMEM((2, 3, HALF, D), BF16),
            pltpu.VMEM((8, ROWS, D), BF16),
            pltpu.VMEM((8, ROWS, D), BF16),
            pltpu.VMEM((8, ROWS, D), BF16),
            pltpu.VMEM((2, 4, ROWS, D), BF16),
            pltpu.VMEM((15, 8, 128), F32),
            pltpu.VMEM((14, 8, 128), F32),
            dma((2, 4, 4)), dma((2, 4, 4)), dma((8, 2)), dma((8, 2)), dma((8,)), dma((8,)), dma((4,)), dma((4,)),
            dma((2, 4)), dma((2, 4)), dma((2, 2, 4)), dma((2, 2, 4)), dma((2, 3)), dma((2, 3)),
            dma((8,)), dma((8,)), dma((2, 4, 2)), dma((2, 4, 2)), dma((14,)), dma((14,)),
        ],
        compiler_params=pltpu.CompilerParams(
            collective_id=0, has_side_effects=True, vmem_limit_bytes=50 * 2**20
        ),
        cost_estimate=pl.CostEstimate(flops=7247757312, bytes_accessed=900000, transcendentals=3 * 2**20),
    )(clip_emb, text_emb[0], positive.reshape(8, 128), log_temp.reshape(1, 1), bias.reshape(1, 1))
    return (
        loss.reshape(()), grad_clip, grad_text[None], grad_temp.reshape(()), grad_bias.reshape(()),
    )


def solution(mesh):
    return jax.shard_map(
        per_device,
        mesh=mesh,
        in_specs=(P(("clip", "text"), None), P("text", "clip", None), P("clip"), P(), P()),
        out_specs=(P(), P(("clip", "text"), None), P("text", "clip", None), P(), P()),
        check_vma=False,
    )
```

time: 449 us -> 78.5 us (0.17)
  waiting for transfers between devices: 221 us -> 0 us
  blocking collectives: 150 us -> 0 us
  Pallas kernels: 0 us -> 67.9 us
  matrix products: 21.3 us -> 0 us
  between operations: 20.5 us -> 7.13 us
  other arithmetic: 12.9 us -> 0 us
  starting transfers between devices: 9.95 us -> 0 us
  local copies, waits for them, and re-layouts: 12.3 us -> 3.27 us
    psum x3 -> x0, blocking collectives: 150 us -> none  [the longest x1 85.1 us: per_device(): lax.psum((loss_part, bias_part, temp_part), ('clip', 'text'))]
    reduce_scatter x2 -> x0, waiting for transfers between devices: 119 us -> none  [the longest x1 61.6 us: per_device(): lax.psum_scatter(clip_part, 'text', scatter_dimension=1, tiled=True)]
    all_gather x2 -> x0, waiting for transfers between devices: 100 us -> none  [the longest x1 58.9 us: per_device(): clip_full = lax.all_gather(clip_emb, 'text', axis=0, tiled=True)]
    pallas_call x0 -> x1, Pallas kernels: none -> 67.9 us  [per_device(): pl.pallas_call(kernel, out_shape=(rows, rows, one, one, one), in_specs=[v...]
    dot_general x3 -> x0, matrix products: 21.3 us -> none  [the longest x1 9.87 us: per_device(): lax.dot_general(clip_unit, text_unit, (((1,), (1,)), ((), ())), preferred...]
    all_to_all x2 -> x0, starting transfers between devices: 9.8 us -> none  [the longest x1 6.23 us: per_device(): lax.all_to_all(text_done, 'clip', split_axis=0, concat_axis=1, tiled=True)]
    mul x4 -> x0, other arithmetic: 9.63 us -> none  [the longest x2 7.43 us: unit_rows(): normal = wide * scale]
    all_gather x2 -> x0, local copies, waits for them, and re-layouts: 5.67 us -> none  [the longest x1 2.83 us: per_device(): text_full = lax.all_gather(text_emb, 'clip', axis=1, tiled=True)[0]]
  transfers between devices with their start and end apart: 6 -> 0, of which waited for: 4 -> 0; matrix products, arithmetic and copies ran while one was open for 6% -> 0% of each run, Pallas kernels for 0% -> 0%
where the time goes in v1:
time: 78.5 us; the launch traced here: 78.3 us
  Pallas kernels  67.9 us (86%)
  between operations  7.13 us (9%)
  local copies, waits for them, and re-layouts  3.27 us (4%)
    pallas_call x1, Pallas kernels, per_device(): pl.pallas_call(kernel, out_shape=(rows, rows, one, one, one), in_specs=[v...  67.9 us
    unnamed x8, local copies, waits for them, and re-layouts  3.27 us

profile of v1, /device:TPU:1, one launch (start us, length us, event | category | flops | bytes accessed | tf_op | source)
XLA Modules:
  0.0 78.3 jit_solution(5998862267530577303)
XLA Ops:
  1.3 0.0 copy-start.2
  1.9 0.0 copy-done.2
  2.0 0.0 copy-start
  2.0 0.9 %copy-done = bf16[64,1152]{1,0:T(8,128)(2,1)S(1)} copy-done((bf16[64,1152]{1,0:T(8,128)(2,1)S(1)}, bf16[64,1152]{1,0:T(8,128)(2,1)}, u32[]{:S(2)}) %copy-start) | copy-done | bytes 147480
  2.9 0.0 copy-start.1
  2.9 0.9 %copy-done.1 = bf16[1,64,1152]{2,1,0:T(8,128)(2,1)S(1)} copy-done((bf16[1,64,1152]{2,1,0:T(8,128)(2,1)S(1)}, bf16[1,64,1152]{2,1,0:T(8,128)(2,1)}, u32[]{:S(2)}) %copy-start.1) | copy-done | bytes 147480
  3.8 67.9 %shard_map.92 = (f32[64,1152]{1,0:T(8,128)S(1)}, f32[64,1152]{1,0:T(8,128)S(1)}, f32[1,1]{1,0:T(1,128)}, f32[1,1]{1,0:T(1,128)}, f32[1,1]{1,0:T(1,128)}) custom-call(bf16[64,1152]{1,0:T(8,128)(2,1)S(1)} %copy-done, bf16[64,1152]{1,0:T(8,128)(2,1)S(1)} %bitcast.11, s32[8,128]{1,0:T(8,128)S(1)} %bitcast.12, f32[1,1]{1,0:T(1,128)} %bitcast.8.log_temp_ref, ...), custom_call_target="tpu_custom_call" | custom-call | flops 7247757312 | bytes 900000 | tf_op jit(solution)/shard_map/pallas_call | solution.py:412
  72.3 0.7 copy.18
  73.1 0.7 copy.19
Async XLA Ops:
  1.3 0.7 copy-start.2
  2.0 0.9 %copy-start = (bf16[64,1152]{1,0:T(8,128)(2,1)S(1)}, bf16[64,1152]{1,0:T(8,128)(2,1)}, u32[]{:S(2)}) copy-start(bf16[64,1152]{1,0:T(8,128)(2,1)} %clip_ref.1) | copy-start | bytes 442372
  2.9 0.9 %copy-start.1 = (bf16[1,64,1152]{2,1,0:T(8,128)(2,1)S(1)}, bf16[1,64,1152]{2,1,0:T(8,128)(2,1)}, u32[]{:S(2)}) copy-start(bf16[1,64,1152]{2,1,0:T(8,128)(2,1)} %param.6) | copy-start | bytes 442372

commit v2 on v1

v2 whole, which is shorter than its diff:
```python
import jax
import jax.numpy as jnp
from jax import lax
from jax.experimental import pallas as pl
from jax.experimental.pallas import tpu as pltpu
from jax.sharding import PartitionSpec as P

MESH = pl.DeviceIdType.MESH
F32 = jnp.float32
BF16 = jnp.bfloat16
LOG2E = 1.4426950408889634
D = 1152
ROWS = 64
HALF = 32
TILE = 1024

CLIP_BLOCK = {0: 0, 1: 1, 3: 2, 2: 3}
TEXT_GROUP = {0: 0, 1: 1, 7: 2, 2: 3, 6: 4, 3: 5, 5: 6, 4: 7}
CHUNK = 16
PARTS = ROWS // CHUNK


def clip_at(half, apart, index):
    return CLIP_BLOCK[apart] * 256 + half * 128 + index * HALF


def text_at(dz, dk):
    return TEXT_GROUP[dz] * 128 + dk * ROWS


def kernel(
    clip_hbm, text_hbm, pos_hbm, log_temp_hbm, bias_hbm,
    grad_clip_ref, grad_text_ref, scalar_ref,
    clip_ref, text_ref, log_temp_ref, bias_ref, clip_norm, clip_scale, text_norm, text_scale,
    clu, txu, posb, posc, colid, dl, gc, gt, acc,
    cs1, cr1, cs2, cr2, cs3, cr3, ks, kr, zs, zr, sums, sumr,
    in_sem,
    clip_send, clip_recv, text_send, text_recv, core_send, core_recv, pos_send, pos_recv,
    c1_send, c1_recv, c2_send, c2_recv, c3_send, c3_recv, k_send, k_recv, z_send, z_recv, s_send, s_recv,
):
    c = lax.axis_index("clip")
    t = lax.axis_index("text")
    x, y, z, k = t // 4, c // 4, (t % 4) * 2 + (c // 2) % 2, c % 2

    def dev(dx=0, dy=0, dz=0, dk=0):
        ax, ay, az, ak = (x + dx) % 4, (y + dy) % 4, (z + dz) % 8, (k + dk) % 2
        return (ay * 4 + (az % 2) * 2 + ak, ax * 4 + az // 2)

    def along(half, step):
        return dev(dy=step) if half == 0 else dev(dx=step)

    def across(half, step):
        return dev(dx=step) if half == 0 else dev(dy=step)

    started = []

    def send(src, dst, ssem, rsem, to):
        copy = pltpu.make_async_remote_copy(
            src_ref=src, dst_ref=dst, send_sem=ssem, recv_sem=rsem, device_id=to, device_id_type=MESH
        )
        copy.start()
        started.append(copy)
        return copy

    peers = [dev(dx=i) for i in (1, 2, 3)] + [dev(dy=i) for i in (1, 2, 3)]
    peers += [dev(dz=i) for i in (1, 7)] + [dev(dk=1)]
    barrier = pltpu.get_barrier_semaphore()
    for peer in peers:
        pl.semaphore_signal(barrier, inc=1, device_id=peer, device_id_type=MESH)
    loads = [
        pltpu.make_async_copy(src, dst, in_sem.at[i])
        for i, (src, dst) in enumerate(
            [(clip_hbm, clip_ref), (text_hbm, text_ref), (pos_hbm, posb.at[0]), (log_temp_hbm, log_temp_ref), (bias_hbm, bias_ref)]
        )
    ]
    for load in loads:
        load.start()

    def unit_rows(ref, scale_ref, norm_ref):
        wide = ref[...].astype(F32)
        scale = lax.rsqrt(jnp.sum(wide * wide, axis=1, keepdims=True) + 1e-06)
        normal = wide * scale
        scale_ref[...] = scale
        norm_ref[...] = normal
        return normal.astype(BF16)

    loads[0].wait()
    clip_unit = unit_rows(clip_ref, clip_scale, clip_norm)
    for half in (0, 1):
        clu[pl.ds(clip_at(half, 0, 0), HALF), :] = clip_unit[half * HALF:(half + 1) * HALF, :]
    loads[1].wait()
    txu[pl.ds(text_at(0, 0), ROWS), :] = unit_rows(text_ref, text_scale, text_norm)
    for load in loads[2:]:
        load.wait()

    pl.semaphore_wait(barrier, len(peers))

    def text_piece(dz, dk, part):
        return txu.at[pl.ds(text_at(dz, dk) + part * CHUNK, CHUNK)]

    text_copy = {}

    def text_hop(src_dz, step, part):
        dst_dz = (src_dz - step) % 8
        text_copy[dst_dz, part] = send(
            text_piece(src_dz, 0, part), text_piece(dst_dz, 0, part),
            text_send.at[dst_dz, part], text_recv.at[dst_dz, part], dev(dz=step),
        )

    core_copy = {}

    def text_core(dz):
        rows = pl.ds(text_at(dz, 0), ROWS)
        core_copy[dz] = [
            send(txu.at[rows], txu.at[pl.ds(text_at(dz, 1), ROWS)], core_send.at[dz], core_recv.at[dz], dev(dk=1))
        ]

    def core_part(dz, half):
        mine, other = [pl.ds(text_at(dz, dk) + half * HALF, HALF) for dk in (0, 1)]
        copy = send(txu.at[mine], txu.at[other], core_send.at[dz + half * 4], core_recv.at[dz + half * 4], dev(dk=1))
        core_copy.setdefault(dz, []).append(copy)

    clip_copy = {}

    def clip_piece(half, apart, index):
        return clu.at[pl.ds(clip_at(half, apart, index), HALF)]

    def clip_first(half, step):
        index = (-step) % 4
        clip_copy[half, 0, index] = send(
            clip_piece(half, 0, 0), clip_piece(half, 0, index),
            clip_send.at[half, 0, index], clip_recv.at[half, 0, index], across(half, step),
        )

    def clip_second(half, src_apart, index, step):
        apart = (src_apart - step) % 4
        clip_copy[half, apart, index] = send(
            clip_piece(half, src_apart, index), clip_piece(half, apart, index),
            clip_send.at[half, apart, index], clip_recv.at[half, apart, index], along(half, step),
        )

    def text_step(distance, part):
        for step in (1, -1):
            dz = -distance % 8 if step == 1 else distance
            at = part if step == 1 else PARTS - 1 - part
            text_copy[dz, at].wait_recv()
            if distance < 3 or (distance == 3 and part < PARTS // 2):
                text_hop(dz, step, at)
            if distance == 4:
                if part == PARTS // 2 - 1:
                    core_part(4, 0 if step == 1 else 1)
            elif part == PARTS - 1:
                text_core(dz)

    def clip_pass(index):
        for half in (0, 1):
            clip_copy[half, 0, index].wait_recv()
            for step in (1, -1) if index < 2 else (-1, 1):
                clip_second(half, 0, index, step)

    def clip_on(index):
        for half in (0, 1):
            if index < 2:
                clip_copy[half, 3, index].wait_recv()
                clip_second(half, 3, index, 1)
            else:
                clip_copy[half, 1, index].wait_recv()
                clip_second(half, 1, index, -1)

    def clip_near():
        for half in (0, 1):
            for index in range(4):
                clip_copy[half, 1 if index < 2 else 3, index].wait_recv()

    def clip_far():
        for half in (0, 1):
            for index in range(4):
                clip_copy[half, 2, index].wait_recv()

    for part in range(PARTS):
        text_hop(0, 1, part)
        text_hop(0, -1, PARTS - 1 - part)
    for step in (1, -1, 2):
        for half in (0, 1):
            clip_first(half, step)
    for half in (0, 1):
        clip_second(half, 0, 0, 1)
        clip_second(half, 0, 0, -1)
    text_core(0)
    pos_copy = [
        send(posb.at[0], posb.at[(-step) % 4], pos_send.at[step], pos_recv.at[step], dev(dy=step)) for step in (1, 2, 3)
    ]

    lane = lax.broadcasted_iota(jnp.int32, (8, 128), 1)
    for dz in range(8):
        az = (z + dz) % 8
        base = (x * 4 + az // 2) * 1024 + (y * 4 + (az % 2) * 2) * ROWS
        ids = jnp.where(lane < ROWS, base + k * ROWS, base + (1 - k) * ROWS) + lane % ROWS
        colid[:, pl.ds(text_at(dz, 0), 128)] = ids.astype(F32)
    temp = jnp.exp(jnp.broadcast_to(log_temp_ref[...], (8, 128)))
    factor = (temp * LOG2E)[0:1, 0:1]
    offset = bias_ref[...] * LOG2E
    acc[...] = jnp.zeros_like(acc)

    def fold(value):
        rows, columns = value.shape
        return jnp.sum(value.reshape(rows // 8, 8, columns // 128, 128), axis=(0, 2))

    def piece(block, first, last):
        rows = pl.ds(block * 256, 256)
        columns = pl.ds(first * 128, (last - first) * 128)
        sims = lax.dot_general(clu[rows, :], txu[columns, :], (((1,), (1,)), ((), ())), preferred_element_type=F32)
        e = jnp.exp2(sims * factor + offset)
        plus = 1.0 + e
        inverse = 1.0 / plus
        mask = posc[rows, :] == colid[0:1, columns]
        dlogit = jnp.where(mask, -inverse, e * inverse)
        acc[0] += fold(jnp.log(plus))
        acc[1] += fold(dlogit)
        acc[2] += fold(dlogit * sims)
        acc[3] += fold(jnp.where(mask, sims, 0.0))
        dl[rows, columns] = dlogit.astype(BF16)

    def positives():
        for copy in pos_copy:
            copy.wait_recv()
        z_hi = z // 2
        row_in = lax.broadcasted_iota(jnp.int32, (HALF, 128), 0)
        lane_in = lax.broadcasted_iota(jnp.int32, (HALF, 128), 1)
        for half in (0, 1):
            hit = lane_in == row_in + ((z_hi % 2) * ROWS + half * HALF)
            for dx in range(4):
                for dy in range(4):
                    apart, index = (dy, dx) if half == 0 else (dx, dy)
                    row = ((x + dx) % 4) * 2 + z_hi // 2
                    values = posb[dy, pl.ds(row, 1), :].astype(F32)
                    posc[pl.ds(clip_at(half, apart, index), HALF), :] = jnp.sum(
                        jnp.where(hit, values, 0.0), axis=1, keepdims=True
                    )

    def text_ready(*groups):
        for dz in groups:
            for copy in core_copy[dz]:
                copy.wait_recv()

    text_step(1, 0)
    clip_pass(1)
    clip_pass(3)
    text_step(1, 1)
    text_step(1, 2)
    clip_pass(2)
    text_step(1, 3)
    positives()
    text_step(2, 0)
    clip_on(0)
    clip_on(3)
    text_step(2, 1)
    text_step(2, 2)
    clip_on(1)
    clip_on(2)
    text_step(2, 3)
    text_ready(0, 1, 7, 2)
    piece(0, 0, 4)
    text_step(3, 0)
    text_step(3, 1)
    clip_near()
    piece(1, 0, 4)
    text_step(3, 2)
    text_step(3, 3)
    piece(2, 0, 4)
    text_ready(6, 3, 5)
    piece(0, 4, 7)
    text_step(4, 0)
    piece(1, 4, 7)
    piece(2, 4, 7)
    text_step(4, 1)
    clip_far()
    piece(3, 0, 4)
    text_ready(4)
    piece(3, 4, 8)
    for i in range(3):
        piece(i, 7, 8)

    def share(slots, targets):
        return [
            send(sums.at[slots[0]], sumr.at[slot], s_send.at[slot], s_recv.at[slot], to)
            for slot, to in zip(slots, targets)
        ]

    def collect(copies, slots, nxt):
        total = sums[slots[0]]
        for copy, slot in zip(copies, slots):
            copy.wait_recv()
            total = total + sumr[slot]
        sums[nxt] = total

    for i in range(4):
        sums[0, pl.ds(i, 1), :] = jnp.sum(acc[i], axis=0, keepdims=True)
    sums[0, pl.ds(4, 4), :] = jnp.zeros((4, 128), F32)
    core_slots, x_slots, y_slots, z_slots = (0,), (1, 2, 3), (4, 5, 6), tuple(range(7, 14))
    core_share = share(core_slots, [dev(dk=1)])

    def text_grad(i):
        rows = pl.ds(i * 256, 256)
        gt[rows, :] = lax.dot_general(dl[:, i * 256:(i + 1) * 256], clu[...], (((0,), (0,)), ((), ())), preferred_element_type=F32)

    def clip_grad(i):
        rows = pl.ds(i * 256, 256)
        gc[rows, :] = lax.dot_general(dl[rows, :], txu[...], (((1,), (0,)), ((), ())), preferred_element_type=F32)

    k_copy = {}

    def to_core(dz):
        ks[dz] = gt[pl.ds(text_at(dz, 1), ROWS), :].astype(BF16)
        k_copy[dz] = send(ks.at[dz], kr.at[dz], k_send.at[dz], k_recv.at[dz], dev(dk=1))

    def text_sum(dz, part):
        rows = pl.ds(part * CHUNK, CHUNK)
        return gt[pl.ds(text_at(dz, 0) + part * CHUNK, CHUNK), :] + kr[dz, rows, :].astype(F32)

    z_copy = {}

    def ring(stage, part):
        for way in (0, 1):
            dz = 4 - stage if way == 0 else 4 + stage
            at = part if way == 0 else PARTS - 1 - part
            rows = pl.ds(at * CHUNK, CHUNK)
            value = text_sum(dz, at)
            if stage > 1 or (stage == 1 and part < PARTS // 2):
                z_copy[way, stage - 1, at].wait_recv()
                value = value + zr[way, stage - 1, rows, :].astype(F32)
            zs[dz, rows, :] = value.astype(BF16)
            z_copy[way, stage, at] = send(
                zs.at[dz, rows], zr.at[way, stage, rows], z_send.at[way, stage, at], z_recv.at[way, stage, at],
                dev(dz=1 if way == 0 else -1),
            )

    def core_back(dz):
        k_copy[dz].wait_recv()

    c1_copy = {}
    c2_copy = {}
    c3_copy = {}

    def clip_r1(*indices):
        for index in indices:
            for half in (0, 1):
                cs1[half, index] = gc[pl.ds(clip_at(half, 2, index), HALF), :].astype(BF16)
                c1_copy[half, index] = send(
                    cs1.at[half, index], cr1.at[half, index], c1_send.at[half, index], c1_recv.at[half, index],
                    along(half, 1 if index < 2 else -1),
                )

    def clip_r2(way, *indices):
        apart = 1 if way == 0 else 3
        for index in indices:
            for half in (0, 1):
                value = gc[pl.ds(clip_at(half, apart, index), HALF), :]
                if (index < 2) == (way == 0):
                    c1_copy[half, index].wait_recv()
                    value = value + cr1[half, index].astype(F32)
                cs2[half, way, index] = value.astype(BF16)
                c2_copy[half, way, index] = send(
                    cs2.at[half, way, index], cr2.at[half, way, index],
                    c2_send.at[half, way, index], c2_recv.at[half, way, index],
                    along(half, 1 if way == 0 else -1),
                )

    def clip_r3(index):
        for half in (0, 1):
            value = gc[pl.ds(clip_at(half, 0, index), HALF), :]
            for way in (0, 1):
                c2_copy[half, way, index].wait_recv()
                value = value + cr2[half, way, index].astype(F32)
            if index == 0:
                gc[pl.ds(clip_at(half, 0, 0), HALF), :] = value
            else:
                cs3[half, index - 1] = value.astype(BF16)
                c3_copy[half, index] = send(
                    cs3.at[half, index - 1], cr3.at[half, index - 1],
                    c3_send.at[half, index - 1], c3_recv.at[half, index - 1], across(half, index),
                )

    text_grad(3)
    to_core(4)
    to_core(5)
    clip_grad(3)
    clip_r1(1, 2)
    clip_r1(0, 3)
    core_back(4)
    ring(0, 0)
    ring(0, 1)
    text_grad(2)
    to_core(3)
    to_core(6)
    clip_grad(1)
    clip_r2(0, 2, 3)
    clip_grad(2)
    clip_r2(1, 1, 0)
    core_back(3)
    core_back(5)
    ring(1, 2)
    ring(1, 3)
    collect(core_share, core_slots, 1)
    x_share = share(x_slots, [dev(dx=i) for i in (1, 2, 3)])
    text_grad(1)
    to_core(2)
    to_core(7)
    ring(1, 0)
    clip_r2(0, 1)
    clip_r2(1, 2)
    ring(1, 1)
    text_grad(0)
    to_core(1)
    to_core(0)
    clip_r2(0, 0)
    clip_r2(1, 3)
    clip_grad(0)
    core_back(2)
    core_back(6)
    ring(2, 2)
    ring(2, 3)
    collect(x_share, x_slots, 4)
    y_share = share(y_slots, [dev(dy=i) for i in (1, 2, 3)])
    ring(2, 0)
    clip_r3(2)
    clip_r3(1)
    ring(2, 1)
    clip_r3(3)
    clip_r3(0)
    core_back(1)
    core_back(7)
    ring(3, 2)
    ring(3, 3)
    ring(3, 0)
    ring(3, 1)
    collect(y_share, y_slots, 7)
    z_share = share(z_slots, [dev(dz=i) for i in range(1, 8)])
    core_back(0)

    def finish(scale, normal, back):
        return scale * (back - normal * jnp.sum(normal * back, axis=1, keepdims=True))

    temp_one = temp[0:1, 0:1]

    def finish_text(part):
        rows = pl.ds(part * CHUNK, CHUNK)
        value = text_sum(0, part)
        for way in (0, 1):
            z_copy[way, 3, part].wait_recv()
            value = value + zr[way, 3, rows, :].astype(F32)
        grad_text_ref[rows, :] = finish(text_scale[rows, :], text_norm[rows, :], temp_one * value)

    def finish_clip(half):
        rows = pl.ds(half * HALF, HALF)
        value = gc[pl.ds(clip_at(half, 0, 0), HALF), :]
        for index in (1, 3, 2):
            c3_copy[half, index].wait_recv()
            value = value + cr3[half, index - 1].astype(F32)
        grad_clip_ref[rows, :] = finish(clip_scale[rows, :], clip_norm[rows, :], temp_one * value)

    for half in (0, 1):
        finish_clip(half)
    for part in range(PARTS):
        finish_text(part)
    collect(z_share, z_slots, 14)

    total = jnp.sum(sums[14], axis=1, keepdims=True)
    pairs = 16384.0
    loss = (total[0:1] - temp_one * total[3:4]) / pairs - bias_ref[...]
    for i, value in enumerate((loss, temp_one * total[2:3] / pairs, total[1:2] / pairs)):
        scalar_ref[pl.ds(i, 1), :] = jnp.broadcast_to(value, (1, 128))

    for copy in started:
        copy.wait_send()


def deliver(grad_clip_in, grad_text_in, scalar_in, grad_clip_ref, grad_text_ref, loss_ref, grad_temp_ref, grad_bias_ref, ones, sem):
    pairs = [(grad_clip_in, grad_clip_ref), (grad_text_in, grad_text_ref)]
    for i, ref in enumerate((loss_ref, grad_temp_ref, grad_bias_ref)):
        ones[i] = scalar_in[pl.ds(i, 1), 0:1]
        pairs.append((ones.at[i], ref))
    copies = [pltpu.make_async_copy(src, dst, sem.at[i]) for i, (src, dst) in enumerate(pairs)]
    for copy in copies:
        copy.start()
    for copy in copies:
        copy.wait()


def per_device(clip_emb, text_emb, positive, log_temp, bias):
    hbm = pl.BlockSpec(memory_space=pltpu.HBM)
    vmem = pl.BlockSpec(memory_space=pltpu.VMEM)
    one = jax.ShapeDtypeStruct((1, 1), F32)
    rows = jax.ShapeDtypeStruct((ROWS, D), F32)
    dma = pltpu.SemaphoreType.DMA
    grad_clip, grad_text, scalars = pl.pallas_call(
        kernel,
        out_shape=(rows, rows, jax.ShapeDtypeStruct((8, 128), F32)),
        in_specs=[hbm] * 5,
        out_specs=(vmem, vmem, vmem),
        scratch_shapes=[
            pltpu.VMEM((ROWS, D), BF16),
            pltpu.VMEM((ROWS, D), BF16),
            pltpu.VMEM((1, 1), F32),
            pltpu.VMEM((1, 1), F32),
            pltpu.VMEM((ROWS, D), F32),
            pltpu.VMEM((ROWS, 1), F32),
            pltpu.VMEM((ROWS, D), F32),
            pltpu.VMEM((ROWS, 1), F32),
            pltpu.VMEM((TILE, D), BF16),
            pltpu.VMEM((TILE, D), BF16),
            pltpu.VMEM((4, 8, 128), jnp.int32),
            pltpu.VMEM((TILE, 1), F32),
            pltpu.VMEM((8, TILE), F32),
            pltpu.VMEM((TILE, TILE), BF16),
            pltpu.VMEM((TILE, D), F32),
            pltpu.VMEM((TILE, D), F32),
            pltpu.VMEM((4, 8, 128), F32),
            pltpu.VMEM((2, 4, HALF, D), BF16),
            pltpu.VMEM((2, 4, HALF, D), BF16),
            pltpu.VMEM((2, 2, 4, HALF, D), BF16),
            pltpu.VMEM((2, 2, 4, HALF, D), BF16),
            pltpu.VMEM((2, 3, HALF, D), BF16),
            pltpu.VMEM((2, 3, HALF, D), BF16),
            pltpu.VMEM((8, ROWS, D), BF16),
            pltpu.VMEM((8, ROWS, D), BF16),
            pltpu.VMEM((8, ROWS, D), BF16),
            pltpu.VMEM((2, 4, ROWS, D), BF16),
            pltpu.VMEM((15, 8, 128), F32),
            pltpu.VMEM((14, 8, 128), F32),
            dma((5,)),
            dma((2, 4, 4)), dma((2, 4, 4)), dma((8, PARTS)), dma((8, PARTS)), dma((9,)), dma((9,)), dma((4,)), dma((4,)),
            dma((2, 4)), dma((2, 4)), dma((2, 2, 4)), dma((2, 2, 4)), dma((2, 3)), dma((2, 3)),
            dma((8,)), dma((8,)), dma((2, 4, PARTS)), dma((2, 4, PARTS)), dma((14,)), dma((14,)),
        ],
        compiler_params=pltpu.CompilerParams(
            collective_id=0, has_side_effects=True, vmem_limit_bytes=50 * 2**20
        ),
        cost_estimate=pl.CostEstimate(flops=7247757312, bytes_accessed=900000, transcendentals=3 * 2**20),
    )(clip_emb, text_emb[0], positive.reshape(8, 128), log_temp.reshape(1, 1), bias.reshape(1, 1))
    grad_clip, grad_text, loss, grad_temp, grad_bias = pl.pallas_call(
        deliver,
        out_shape=(rows, rows, one, one, one),
        in_specs=[vmem] * 3,
        out_specs=(hbm,) * 5,
        scratch_shapes=[pltpu.VMEM((3, 1, 1), F32), dma((5,))],
    )(grad_clip, grad_text, scalars)
    return (
        loss.reshape(()), grad_clip, grad_text[None], grad_temp.reshape(()), grad_bias.reshape(()),
    )


def solution(mesh):
    return jax.shard_map(
        per_device,
        mesh=mesh,
        in_specs=(P(("clip", "text"), None), P("text", "clip", None), P("clip"), P(), P()),
        out_specs=(P(), P(("clip", "text"), None), P("text", "clip", None), P(), P()),
        check_vma=False,
    )
```

time: 78.5 us -> 67.6 us (0.86)
  Pallas kernels: 67.9 us -> 61.4 us
  between operations: 7.13 us -> 2.13 us
    pallas_call x1 -> x2, Pallas kernels: 67.9 us -> 61.4 us  [the longest x1 59.5 us: per_device(): pl.pallas_call(kernel, out_shape=(rows, rows, jax.ShapeDtypeStruct((8, 12...]
    unnamed x8 -> x12, local copies, waits for them, and re-layouts: 3.27 us -> 3.84 us
where the time goes in v2:
time: 67.6 us; the launch traced here: 67.4 us
  Pallas kernels  61.4 us (91%)
  local copies, waits for them, and re-layouts  3.84 us (6%)
  between operations  2.13 us (3%)
    pallas_call x1, Pallas kernels, per_device(): pl.pallas_call(kernel, out_shape=(rows, rows, jax.ShapeDtypeStruct((8, 12...  59.5 us
    unnamed x12, local copies, waits for them, and re-layouts  3.84 us
    pallas_call x1, Pallas kernels, per_device(): pl.pallas_call(deliver, out_shape=(rows, rows, one, one, one), in_specs=[...  1.91 us

profile of v2, /device:TPU:1, one launch (start us, length us, event | category | flops | bytes accessed | tf_op | source)
XLA Modules:
  0.0 67.4 jit_solution(3272949183893314810)
XLA Ops:
  1.3 0.0 copy-start.5
  1.9 0.0 copy-done.5
  2.0 0.0 copy-start.3
  2.0 0.9 %copy-done.3 = bf16[64,1152]{1,0:T(8,128)(2,1)S(1)} copy-done((bf16[64,1152]{1,0:T(8,128)(2,1)S(1)}, bf16[64,1152]{1,0:T(8,128)(2,1)}, u32[]{:S(2)}) %copy-start.3) | copy-done | bytes 147480
  2.9 0.0 copy-start.4
  2.9 0.9 %copy-done.4 = bf16[1,64,1152]{2,1,0:T(8,128)(2,1)S(1)} copy-done((bf16[1,64,1152]{2,1,0:T(8,128)(2,1)S(1)}, bf16[1,64,1152]{2,1,0:T(8,128)(2,1)}, u32[]{:S(2)}) %copy-start.4) | copy-done | bytes 147480
  3.8 59.5 %shard_map.92 = (f32[64,1152]{1,0:T(8,128)S(1)}, f32[64,1152]{1,0:T(8,128)S(1)}, f32[8,128]{1,0:T(8,128)S(1)}) custom-call(bf16[64,1152]{1,0:T(8,128)(2,1)S(1)} %copy-done.3, bf16[64,1152]{1,0:T(8,128)(2,1)S(1)} %bitcast.10, s32[8,128]{1,0:T(8,128)S(1)} %bitcast.11, f32[1,1]{1,0:T(1,128)} %bitcast.8.log_temp_hbm, f32[1,1]{1,0:T(1,128)} %bitcast.9.bias_hbm), custom_call_target="tpu_custom_call" | custom-call | flops 7247757312 | bytes 900000 | tf_op jit(solution)/shard_map/pallas_call | solution.py:496
  63.3 0.0 copy-start
  63.3 0.7 %copy-done = f32[64,1152]{1,0:T(8,128)} copy-done((f32[64,1152]{1,0:T(8,128)}, f32[64,1152]{1,0:T(8,128)S(1)}, u32[]{:S(2)}) %copy-start) | copy-done | bytes 294936
  64.0 0.0 copy-start.1
  64.0 0.7 %copy-done.1 = f32[64,1152]{1,0:T(8,128)} copy-done((f32[64,1152]{1,0:T(8,128)}, f32[64,1152]{1,0:T(8,128)S(1)}, u32[]{:S(2)}) %copy-start.1) | copy-done | bytes 294936
  64.7 0.0 copy-start.2
  64.7 0.6 copy-done.2
  65.3 1.9 %shard_map.93 = (f32[64,1152]{1,0:T(8,128)}, f32[64,1152]{1,0:T(8,128)}, f32[1,1]{1,0:T(1,128)}, f32[1,1]{1,0:T(1,128)}, f32[1,1]{1,0:T(1,128)}) custom-call(f32[64,1152]{1,0:T(8,128)} %copy-done, f32[64,1152]{1,0:T(8,128)} %copy-done.1, f32[8,128]{1,0:T(8,128)} %copy-done.2), custom_call_target="tpu_custom_call" | custom-call | tf_op jit(solution)/shard_map/pallas_call | solution.py:541
Async XLA Ops:
  1.3 0.7 %copy-start.5 = (s32[1024]{0:T(1024)S(1)}, s32[1024]{0:T(1024)}, u32[]{:S(2)}) copy-start(s32[1024]{0:T(1024)} %param.7) | copy-start | bytes 12292
  2.0 0.9 %copy-start.3 = (bf16[64,1152]{1,0:T(8,128)(2,1)S(1)}, bf16[64,1152]{1,0:T(8,128)(2,1)}, u32[]{:S(2)}) copy-start(bf16[64,1152]{1,0:T(8,128)(2,1)} %clip_hbm.1) | copy-start | bytes 442372
  2.9 0.9 %copy-start.4 = (bf16[1,64,1152]{2,1,0:T(8,128)(2,1)S(1)}, bf16[1,64,1152]{2,1,0:T(8,128)(2,1)}, u32[]{:S(2)}) copy-start(bf16[1,64,1152]{2,1,0:T(8,128)(2,1)} %param.6) | copy-start | bytes 442372
  63.3 0.7 %copy-start = (f32[64,1152]{1,0:T(8,128)}, f32[64,1152]{1,0:T(8,128)S(1)}, u32[]{:S(2)}) copy-start(f32[64,1152]{1,0:T(8,128)S(1)} %get-tuple-element.13.grad_clip_in) | copy-start | bytes 884740
  64.0 0.7 %copy-start.1 = (f32[64,1152]{1,0:T(8,128)}, f32[64,1152]{1,0:T(8,128)S(1)}, u32[]{:S(2)}) copy-start(f32[64,1152]{1,0:T(8,128)S(1)} %get-tuple-element.14.grad_text_in) | copy-start | bytes 884740
  64.7 0.6 copy-start.2

commit v3 on v2

--- a/solution.py
+++ b/solution.py
@@ -29,12 +29,11 @@
 
 
 def kernel(
-    clip_hbm, text_hbm, pos_hbm, log_temp_hbm, bias_hbm,
+    emb_ref, pos_ref, given_ref,
     grad_clip_ref, grad_text_ref, scalar_ref,
-    clip_ref, text_ref, log_temp_ref, bias_ref, clip_norm, clip_scale, text_norm, text_scale,
+    clip_norm, clip_scale, text_norm, text_scale,
     clu, txu, posb, posc, colid, dl, gc, gt, acc,
     cs1, cr1, cs2, cr2, cs3, cr3, ks, kr, zs, zr, sums, sumr,
-    in_sem,
     clip_send, clip_recv, text_send, text_recv, core_send, core_recv, pos_send, pos_recv,
     c1_send, c1_recv, c2_send, c2_recv, c3_send, c3_recv, k_send, k_recv, z_send, z_recv, s_send, s_recv,
 ):
@@ -67,31 +66,19 @@
     barrier = pltpu.get_barrier_semaphore()
     for peer in peers:
         pl.semaphore_signal(barrier, inc=1, device_id=peer, device_id_type=MESH)
-    loads = [
-        pltpu.make_async_copy(src, dst, in_sem.at[i])
-        for i, (src, dst) in enumerate(
-            [(clip_hbm, clip_ref), (text_hbm, text_ref), (pos_hbm, posb.at[0]), (log_temp_hbm, log_temp_ref), (bias_hbm, bias_ref)]
-        )
-    ]
-    for load in loads:
-        load.start()
-
-    def unit_rows(ref, scale_ref, norm_ref):
-        wide = ref[...].astype(F32)
+    def unit_rows(first, scale_ref, norm_ref):
+        wide = emb_ref[pl.ds(first, ROWS), :].astype(F32)
         scale = lax.rsqrt(jnp.sum(wide * wide, axis=1, keepdims=True) + 1e-06)
         normal = wide * scale
         scale_ref[...] = scale
         norm_ref[...] = normal
         return normal.astype(BF16)
 
-    loads[0].wait()
-    clip_unit = unit_rows(clip_ref, clip_scale, clip_norm)
+    clip_unit = unit_rows(0, clip_scale, clip_norm)
     for half in (0, 1):
         clu[pl.ds(clip_at(half, 0, 0), HALF), :] = clip_unit[half * HALF:(half + 1) * HALF, :]
-    loads[1].wait()
-    txu[pl.ds(text_at(0, 0), ROWS), :] = unit_rows(text_ref, text_scale, text_norm)
-    for load in loads[2:]:
-        load.wait()
+    txu[pl.ds(text_at(0, 0), ROWS), :] = unit_rows(ROWS, text_scale, text_norm)
+    posb[0] = pos_ref[...]
 
     pl.semaphore_wait(barrier, len(peers))
 
@@ -197,17 +184,19 @@
         base = (x * 4 + az // 2) * 1024 + (y * 4 + (az % 2) * 2) * ROWS
         ids = jnp.where(lane < ROWS, base + k * ROWS, base + (1 - k) * ROWS) + lane % ROWS
         colid[:, pl.ds(text_at(dz, 0), 128)] = ids.astype(F32)
-    temp = jnp.exp(jnp.broadcast_to(log_temp_ref[...], (8, 128)))
-    factor = (temp * LOG2E)[0:1, 0:1]
-    offset = bias_ref[...] * LOG2E
+    temp = jnp.exp(given_ref[0:1, 0:1])
+    bias = given_ref[1:2, 0:1]
+    factor = temp * LOG2E
+    offset = bias * LOG2E
     acc[...] = jnp.zeros_like(acc)
 
     def fold(value):
         rows, columns = value.shape
-        return jnp.sum(value.reshape(rows // 8, 8, columns // 128, 128), axis=(0, 2))
-
-    def piece(block, first, last):
-        rows = pl.ds(block * 256, 256)
+        wide = jnp.sum(value.reshape(rows // 8, 8, columns), axis=0)
+        return sum(wide[:, at:at + 128] for at in range(0, columns, 128))
+
+    def piece(top, bottom, first, last):
+        rows = pl.ds(top * 256, (bottom - top) * 256)
         columns = pl.ds(first * 128, (last - first) * 128)
         sims = lax.dot_general(clu[rows, :], txu[columns, :], (((1,), (1,)), ((), ())), preferred_element_type=F32)
         e = jnp.exp2(sims * factor + offset)
@@ -215,11 +204,24 @@
         inverse = 1.0 / plus
         mask = posc[rows, :] == colid[0:1, columns]
         dlogit = jnp.where(mask, -inverse, e * inverse)
-        acc[0] += fold(jnp.log(plus))
+        four = plus.reshape(4, plus.shape[0] // 4, plus.shape[1])
+        acc[0] += fold(jnp.log((four[0] * four[1]) * (four[2] * four[3])))
         acc[1] += fold(dlogit)
         acc[2] += fold(dlogit * sims)
         acc[3] += fold(jnp.where(mask, sims, 0.0))
         dl[rows, columns] = dlogit.astype(BF16)
+
+    def text_grad(first, last, top=0, bottom=4):
+        rows = pl.ds(first * 128, (last - first) * 128)
+        over = pl.ds(top * 256, (bottom - top) * 256)
+        part = lax.dot_general(dl[over, rows], clu[over, :], (((0,), (0,)), ((), ())), preferred_element_type=F32)
+        gt[rows, :] = part if top == 0 else gt[rows, :] + part
+
+    def clip_grad(block, first=0, last=8):
+        rows = pl.ds(block * 256, 256)
+        over = pl.ds(first * 128, (last - first) * 128)
+        part = lax.dot_general(dl[rows, over], txu[over, :], (((1,), (0,)), ((), ())), preferred_element_type=F32)
+        gc[rows, :] = part if first == 0 else gc[rows, :] + part
 
     def positives():
         for copy in pos_copy:
@@ -260,26 +262,22 @@
     clip_on(2)
     text_step(2, 3)
     text_ready(0, 1, 7, 2)
-    piece(0, 0, 4)
+    piece(0, 1, 0, 4)
     text_step(3, 0)
     text_step(3, 1)
     clip_near()
-    piece(1, 0, 4)
+    piece(1, 3, 0, 4)
     text_step(3, 2)
     text_step(3, 3)
-    piece(2, 0, 4)
-    text_ready(6, 3, 5)
-    piece(0, 4, 7)
+    clip_grad(0, 0, 4)
+    clip_grad(1, 0, 4)
+    clip_grad(2, 0, 4)
     text_step(4, 0)
-    piece(1, 4, 7)
-    piece(2, 4, 7)
     text_step(4, 1)
+    text_ready(6, 3, 5, 4)
+    piece(0, 3, 4, 8)
     clip_far()
-    piece(3, 0, 4)
-    text_ready(4)
-    piece(3, 4, 8)
-    for i in range(3):
-        piece(i, 7, 8)
+    piece(3, 4, 0, 8)
 
     def share(slots, targets):
         return [
@@ -294,19 +292,12 @@
             total = total + sumr[slot]
         sums[nxt] = total
 
-    for i in range(4):
-        sums[0, pl.ds(i, 1), :] = jnp.sum(acc[i], axis=0, keepdims=True)
-    sums[0, pl.ds(4, 4), :] = jnp.zeros((4, 128), F32)
     core_slots, x_slots, y_slots, z_slots = (0,), (1, 2, 3), (4, 5, 6), tuple(range(7, 14))
-    core_share = share(core_slots, [dev(dk=1)])
-
-    def text_grad(i):
-        rows = pl.ds(i * 256, 256)
-        gt[rows, :] = lax.dot_general(dl[:, i * 256:(i + 1) * 256], clu[...], (((0,), (0,)), ((), ())), preferred_element_type=F32)
-
-    def clip_grad(i):
-        rows = pl.ds(i * 256, 256)
-        gc[rows, :] = lax.dot_general(dl[rows, :], txu[...], (((1,), (0,)), ((), ())), preferred_element_type=F32)
+
+    def first_sums():
+        for i in range(4):
+            sums[0, pl.ds(i, 1), :] = jnp.sum(acc[i], axis=0, keepdims=True)
+        sums[0, pl.ds(4, 4), :] = jnp.zeros((4, 128), F32)
 
     k_copy = {}
 
@@ -381,7 +372,7 @@
                     c3_send.at[half, index - 1], c3_recv.at[half, index - 1], across(half, index),
                 )
 
-    text_grad(3)
+    text_grad(6, 8)
     to_core(4)
     to_core(5)
     clip_grad(3)
@@ -390,12 +381,14 @@
     core_back(4)
     ring(0, 0)
     ring(0, 1)
-    text_grad(2)
+    first_sums()
+    core_share = share(core_slots, [dev(dk=1)])
+    text_grad(4, 6)
     to_core(3)
     to_core(6)
-    clip_grad(1)
+    clip_grad(1, 4)
     clip_r2(0, 2, 3)
-    clip_grad(2)
+    clip_grad(2, 4)
     clip_r2(1, 1, 0)
     core_back(3)
     core_back(5)
@@ -403,29 +396,31 @@
     ring(1, 3)
     collect(core_share, core_slots, 1)
     x_share = share(x_slots, [dev(dx=i) for i in (1, 2, 3)])
-    text_grad(1)
+    text_grad(2, 4)
     to_core(2)
     to_core(7)
     ring(1, 0)
     clip_r2(0, 1)
     clip_r2(1, 2)
     ring(1, 1)
-    text_grad(0)
-    to_core(1)
-    to_core(0)
     clip_r2(0, 0)
     clip_r2(1, 3)
-    clip_grad(0)
+    collect(x_share, x_slots, 4)
+    y_share = share(y_slots, [dev(dy=i) for i in (1, 2, 3)])
+    clip_grad(0, 4)
     core_back(2)
     core_back(6)
     ring(2, 2)
     ring(2, 3)
-    collect(x_share, x_slots, 4)
-    y_share = share(y_slots, [dev(dy=i) for i in (1, 2, 3)])
+    text_grad(0, 2)
+    to_core(1)
+    to_core(0)
     ring(2, 0)
     clip_r3(2)
     clip_r3(1)
     ring(2, 1)
+    collect(y_share, y_slots, 7)
+    z_share = share(z_slots, [dev(dz=i) for i in range(1, 8)])
     clip_r3(3)
     clip_r3(0)
     core_back(1)
@@ -434,14 +429,10 @@
     ring(3, 3)
     ring(3, 0)
     ring(3, 1)
-    collect(y_share, y_slots, 7)
-    z_share = share(z_slots, [dev(dz=i) for i in range(1, 8)])
     core_back(0)
 
     def finish(scale, normal, back):
         return scale * (back - normal * jnp.sum(normal * back, axis=1, keepdims=True))
-
-    temp_one = temp[0:1, 0:1]
 
     def finish_text(part):
         rows = pl.ds(part * CHUNK, CHUNK)
@@ -449,7 +440,7 @@
         for way in (0, 1):
             z_copy[way, 3, part].wait_recv()
             value = value + zr[way, 3, rows, :].astype(F32)
-        grad_text_ref[rows, :] = finish(text_scale[rows, :], text_norm[rows, :], temp_one * value)
+        grad_text_ref[rows, :] = finish(text_scale[rows, :], text_norm[rows, :], value)
 
     def finish_clip(half):
         rows = pl.ds(half * HALF, HALF)
@@ -457,7 +448,7 @@
         for index in (1, 3, 2):
             c3_copy[half, index].wait_recv()
             value = value + cr3[half, index - 1].astype(F32)
-        grad_clip_ref[rows, :] = finish(clip_scale[rows, :], clip_norm[rows, :], temp_one * value)
+        grad_clip_ref[rows, :] = finish(clip_scale[rows, :], clip_norm[rows, :], value)
 
     for half in (0, 1):
         finish_clip(half)
@@ -467,42 +458,25 @@
 
     total = jnp.sum(sums[14], axis=1, keepdims=True)
     pairs = 16384.0
-    loss = (total[0:1] - temp_one * total[3:4]) / pairs - bias_ref[...]
-    for i, value in enumerate((loss, temp_one * total[2:3] / pairs, total[1:2] / pairs)):
+    loss = (total[0:1] - temp * total[3:4]) / pairs - bias
+    for i, value in enumerate((loss, temp * total[2:3] / pairs, total[1:2] / pairs)):
         scalar_ref[pl.ds(i, 1), :] = jnp.broadcast_to(value, (1, 128))
 
     for copy in started:
         copy.wait_send()
 
 
-def deliver(grad_clip_in, grad_text_in, scalar_in, grad_clip_ref, grad_text_ref, loss_ref, grad_temp_ref, grad_bias_ref, ones, sem):
-    pairs = [(grad_clip_in, grad_clip_ref), (grad_text_in, grad_text_ref)]
-    for i, ref in enumerate((loss_ref, grad_temp_ref, grad_bias_ref)):
-        ones[i] = scalar_in[pl.ds(i, 1), 0:1]
-        pairs.append((ones.at[i], ref))
-    copies = [pltpu.make_async_copy(src, dst, sem.at[i]) for i, (src, dst) in enumerate(pairs)]
-    for copy in copies:
-        copy.start()
-    for copy in copies:
-        copy.wait()
-
-
 def per_device(clip_emb, text_emb, positive, log_temp, bias):
-    hbm = pl.BlockSpec(memory_space=pltpu.HBM)
     vmem = pl.BlockSpec(memory_space=pltpu.VMEM)
-    one = jax.ShapeDtypeStruct((1, 1), F32)
     rows = jax.ShapeDtypeStruct((ROWS, D), F32)
     dma = pltpu.SemaphoreType.DMA
+    given = jnp.where(lax.broadcasted_iota(jnp.int32, (8, 128), 0) == 0, log_temp, bias)
     grad_clip, grad_text, scalars = pl.pallas_call(
         kernel,
         out_shape=(rows, rows, jax.ShapeDtypeStruct((8, 128), F32)),
-        in_specs=[hbm] * 5,
+        in_specs=[vmem] * 3,
         out_specs=(vmem, vmem, vmem),
         scratch_shapes=[
-            pltpu.VMEM((ROWS, D), BF16),
-            pltpu.VMEM((ROWS, D), BF16),
-            pltpu.VMEM((1, 1), F32),
-            pltpu.VMEM((1, 1), F32),
             pltpu.VMEM((ROWS, D), F32),
             pltpu.VMEM((ROWS, 1), F32),
             pltpu.VMEM((ROWS, D), F32),
@@ -528,7 +502,6 @@
             pltpu.VMEM((2, 4, ROWS, D), BF16),
             pltpu.VMEM((15, 8, 128), F32),
             pltpu.VMEM((14, 8, 128), F32),
-            dma((5,)),
             dma((2, 4, 4)), dma((2, 4, 4)), dma((8, PARTS)), dma((8, PARTS)), dma((9,)), dma((9,)), dma((4,)), dma((4,)),
             dma((2, 4)), dma((2, 4)), dma((2, 2, 4)), dma((2, 2, 4)), dma((2, 3)), dma((2, 3)),
             dma((8,)), dma((8,)), dma((2, 4, PARTS)), dma((2, 4, PARTS)), dma((14,)), dma((14,)),
@@ -537,17 +510,10 @@
             collective_id=0, has_side_effects=True, vmem_limit_bytes=50 * 2**20
         ),
         cost_estimate=pl.CostEstimate(flops=7247757312, bytes_accessed=900000, transcendentals=3 * 2**20),
-    )(clip_emb, text_emb[0], positive.reshape(8, 128), log_temp.reshape(1, 1), bias.reshape(1, 1))
-    grad_clip, grad_text, loss, grad_temp, grad_bias = pl.pallas_call(
-        deliver,
-        out_shape=(rows, rows, one, one, one),
-        in_specs=[vmem] * 3,
-        out_specs=(hbm,) * 5,
-        scratch_shapes=[pltpu.VMEM((3, 1, 1), F32), dma((5,))],
-    )(grad_clip, grad_text, scalars)
-    return (
-        loss.reshape(()), grad_clip, grad_text[None], grad_temp.reshape(()), grad_bias.reshape(()),
-    )
+    )(jnp.concatenate([clip_emb, text_emb[0]]), positive.reshape(8, 128), given)
+    temp = jnp.exp(log_temp)
+    grad_clip, grad_text = lax.optimization_barrier((temp * grad_clip, temp * grad_text))
+    return scalars[0, 0], grad_clip, grad_text[None], scalars[1, 0], scalars[2, 0]
 
 
 def solution(mesh):

time: 67.6 us -> 60 us (0.89)
  Pallas kernels: 61.4 us -> 55.4 us
  local copies, waits for them, and re-layouts: 3.84 us -> 0.6 us
  other arithmetic: 0 us -> 1.87 us
    pallas_call x1, Pallas kernels: 59.5 us -> 55.4 us  [per_device(): pl.pallas_call(kernel, out_shape=(rows, rows, jax.ShapeDtypeStruct((8, 12...]
    unnamed x12 -> x2, local copies, waits for them, and re-layouts: 3.84 us -> 0.01 us
    pallas_call x1 -> x0, Pallas kernels: 1.91 us -> none  [per_device(): pl.pallas_call(deliver, out_shape=(rows, rows, one, one, one), in_specs=[...]
    concatenate x0 -> x1, other arithmetic: none -> 1.02 us  [per_device(): jnp.concatenate([clip_emb, text_emb[0]])]
    mul x0 -> x1, other arithmetic: none -> 0.85 us  [per_device(): temp * grad_text]
where the time goes in v3:
time: 60 us; the launch traced here: 59.9 us
  Pallas kernels  55.4 us (92%)
  between operations  1.99 us (3%)
  other arithmetic  1.87 us (3%)
  local copies, waits for them, and re-layouts  0.6 us (1%)
    pallas_call x1, Pallas kernels, per_device(): pl.pallas_call(kernel, out_shape=(rows, rows, jax.ShapeDtypeStruct((8, 12...  55.4 us

profile of v3, /device:TPU:1, one launch (start us, length us, event | category | flops | bytes accessed | tf_op | source)
XLA Modules:
  0.0 59.9 jit_solution(16238267016673770858)
XLA Ops:
  2.0 0.1 iota.7.given_ref
  2.0 0.0 copy-start
  2.0 1.0 %pad_maximum_fusion.emb_ref = bf16[128,1152]{1,0:T(8,128)(2,1)S(1)} fusion(bf16[64,1152]{1,0:T(8,128)(2,1)} %bitcast.8, bf16[64,1152]{1,0:T(8,128)(2,1)} %param.5), kind=kLoop, calls=%fused_computation | loop fusion | flops 589824 | bytes 589824 | tf_op jit(solution)/shard_map/concatenate | solution.py:513
  3.1 0.0 copy-done
  3.1 55.4 %shard_map.92 = (f32[64,1152]{1,0:T(8,128)S(1)}, f32[64,1152]{1,0:T(8,128)S(1)}, f32[8,128]{1,0:T(8,128)S(1)}) custom-call(bf16[128,1152]{1,0:T(8,128)(2,1)S(1)} %pad_maximum_fusion.emb_ref, s32[8,128]{1,0:T(8,128)S(1)} %bitcast.6, f32[8,128]{1,0:T(8,128)S(1)} %iota.7.given_ref), custom_call_target="tpu_custom_call" | custom-call | flops 7247757312 | bytes 900000 | tf_op jit(solution)/shard_map/pallas_call | solution.py:474
  58.5 0.5 fusion
  59.0 0.9 %broadcast_multiply_fusion = (f32[64,1152]{1,0:T(8,128)}, f32[64,1152]{1,0:T(8,128)}) fusion(f32[64,1152]{1,0:T(8,128)S(1)} %get-tuple-element.12, f32[]{:T(128)S(6)} %exp.3, f32[64,1152]{1,0:T(8,128)S(1)} %get-tuple-element.11), kind=kLoop, calls=%fused_computation.1 | loop fusion | flops 147456 | bytes 1179652 | tf_op jit(solution)/shard_map/mul | solution.py:515
  (1 shorter events, 0.0 us)
Async XLA Ops:
  2.0 1.0 %copy-start = (s32[1024]{0:T(1024)S(1)}, s32[1024]{0:T(1024)}, u32[]{:S(2)}) copy-start(s32[1024]{0:T(1024)} %param.7) | copy-start | bytes 12292

commit v4 on v3

--- a/solution.py
+++ b/solution.py
@@ -29,7 +29,7 @@
 
 
 def kernel(
-    emb_ref, pos_ref, given_ref,
+    emb_ref, pos_ref, log_temp_ref, bias_ref,
     grad_clip_ref, grad_text_ref, scalar_ref,
     clip_norm, clip_scale, text_norm, text_scale,
     clu, txu, posb, posc, colid, dl, gc, gt, acc,
@@ -164,12 +164,12 @@
             for index in range(4):
                 clip_copy[half, 2, index].wait_recv()
 
+    for step in (1, -1, 2):
+        for half in (0, 1):
+            clip_first(half, step)
     for part in range(PARTS):
         text_hop(0, 1, part)
         text_hop(0, -1, PARTS - 1 - part)
-    for step in (1, -1, 2):
-        for half in (0, 1):
-            clip_first(half, step)
     for half in (0, 1):
         clip_second(half, 0, 0, 1)
         clip_second(half, 0, 0, -1)
@@ -184,8 +184,8 @@
         base = (x * 4 + az // 2) * 1024 + (y * 4 + (az % 2) * 2) * ROWS
         ids = jnp.where(lane < ROWS, base + k * ROWS, base + (1 - k) * ROWS) + lane % ROWS
         colid[:, pl.ds(text_at(dz, 0), 128)] = ids.astype(F32)
-    temp = jnp.exp(given_ref[0:1, 0:1])
-    bias = given_ref[1:2, 0:1]
+    temp = jnp.exp(log_temp_ref[...])
+    bias = bias_ref[...]
     factor = temp * LOG2E
     offset = bias * LOG2E
     acc[...] = jnp.zeros_like(acc)
@@ -252,7 +252,6 @@
     text_step(1, 2)
     clip_pass(2)
     text_step(1, 3)
-    positives()
     text_step(2, 0)
     clip_on(0)
     clip_on(3)
@@ -261,6 +260,7 @@
     clip_on(1)
     clip_on(2)
     text_step(2, 3)
+    positives()
     text_ready(0, 1, 7, 2)
     piece(0, 1, 0, 4)
     text_step(3, 0)
@@ -272,12 +272,14 @@
     clip_grad(0, 0, 4)
     clip_grad(1, 0, 4)
     clip_grad(2, 0, 4)
+    text_ready(6, 3, 5)
+    piece(0, 3, 4, 7)
     text_step(4, 0)
     text_step(4, 1)
-    text_ready(6, 3, 5, 4)
-    piece(0, 3, 4, 8)
     clip_far()
-    piece(3, 4, 0, 8)
+    piece(3, 4, 0, 7)
+    text_ready(4)
+    piece(0, 4, 7, 8)
 
     def share(slots, targets):
         return [
@@ -372,9 +374,8 @@
                     c3_send.at[half, index - 1], c3_recv.at[half, index - 1], across(half, index),
                 )
 
-    text_grad(6, 8)
+    text_grad(7, 8)
     to_core(4)
-    to_core(5)
     clip_grad(3)
     clip_r1(1, 2)
     clip_r1(0, 3)
@@ -383,9 +384,9 @@
     ring(0, 1)
     first_sums()
     core_share = share(core_slots, [dev(dk=1)])
-    text_grad(4, 6)
+    text_grad(5, 7)
     to_core(3)
-    to_core(6)
+    to_core(5)
     clip_grad(1, 4)
     clip_r2(0, 2, 3)
     clip_grad(2, 4)
@@ -396,9 +397,9 @@
     ring(1, 3)
     collect(core_share, core_slots, 1)
     x_share = share(x_slots, [dev(dx=i) for i in (1, 2, 3)])
-    text_grad(2, 4)
+    text_grad(3, 5)
     to_core(2)
-    to_core(7)
+    to_core(6)
     ring(1, 0)
     clip_r2(0, 1)
     clip_r2(1, 2)
@@ -412,24 +413,27 @@
     core_back(6)
     ring(2, 2)
     ring(2, 3)
-    text_grad(0, 2)
+    text_grad(0, 3)
     to_core(1)
+    to_core(7)
     to_core(0)
     ring(2, 0)
-    clip_r3(2)
-    clip_r3(1)
     ring(2, 1)
-    collect(y_share, y_slots, 7)
-    z_share = share(z_slots, [dev(dz=i) for i in range(1, 8)])
-    clip_r3(3)
-    clip_r3(0)
     core_back(1)
     core_back(7)
     ring(3, 2)
+    collect(y_share, y_slots, 7)
+    z_share = share(z_slots, [dev(dz=i) for i in range(1, 8)])
+    clip_r3(2)
+    clip_r3(1)
     ring(3, 3)
     ring(3, 0)
+    clip_r3(3)
+    clip_r3(0)
     ring(3, 1)
     core_back(0)
+
+    half_temp = 0.5 * temp
 
     def finish(scale, normal, back):
         return scale * (back - normal * jnp.sum(normal * back, axis=1, keepdims=True))
@@ -440,7 +444,7 @@
         for way in (0, 1):
             z_copy[way, 3, part].wait_recv()
             value = value + zr[way, 3, rows, :].astype(F32)
-        grad_text_ref[rows, :] = finish(text_scale[rows, :], text_norm[rows, :], value)
+        grad_text_ref[rows, :] = finish(half_temp * text_scale[rows, :], text_norm[rows, :], value)
 
     def finish_clip(half):
         rows = pl.ds(half * HALF, HALF)
@@ -448,7 +452,7 @@
         for index in (1, 3, 2):
             c3_copy[half, index].wait_recv()
             value = value + cr3[half, index - 1].astype(F32)
-        grad_clip_ref[rows, :] = finish(clip_scale[rows, :], clip_norm[rows, :], value)
+        grad_clip_ref[rows, :] = finish(half_temp * clip_scale[rows, :], clip_norm[rows, :], value)
 
     for half in (0, 1):
         finish_clip(half)
@@ -470,11 +474,10 @@
     vmem = pl.BlockSpec(memory_space=pltpu.VMEM)
     rows = jax.ShapeDtypeStruct((ROWS, D), F32)
     dma = pltpu.SemaphoreType.DMA
-    given = jnp.where(lax.broadcasted_iota(jnp.int32, (8, 128), 0) == 0, log_temp, bias)
     grad_clip, grad_text, scalars = pl.pallas_call(
         kernel,
         out_shape=(rows, rows, jax.ShapeDtypeStruct((8, 128), F32)),
-        in_specs=[vmem] * 3,
+        in_specs=[vmem] * 4,
         out_specs=(vmem, vmem, vmem),
         scratch_shapes=[
             pltpu.VMEM((ROWS, D), F32),
@@ -510,9 +513,8 @@
             collective_id=0, has_side_effects=True, vmem_limit_bytes=50 * 2**20
         ),
         cost_estimate=pl.CostEstimate(flops=7247757312, bytes_accessed=900000, transcendentals=3 * 2**20),
-    )(jnp.concatenate([clip_emb, text_emb[0]]), positive.reshape(8, 128), given)
-    temp = jnp.exp(log_temp)
-    grad_clip, grad_text = lax.optimization_barrier((temp * grad_clip, temp * grad_text))
+    )(jnp.concatenate([clip_emb, text_emb[0]]), positive.reshape(8, 128), log_temp.reshape(1, 1), bias.reshape(1, 1))
+    grad_clip, grad_text = lax.optimization_barrier((2.0 * grad_clip, 2.0 * grad_text))
     return scalars[0, 0], grad_clip, grad_text[None], scalars[1, 0], scalars[2, 0]
 
 

time: 60 us -> 59.4 us (0.990)
  no operation moved by 1% of the time
where the time goes in v4:
time: 59.4 us; the launch traced here: 59.3 us
  Pallas kernels  54.9 us (92%)
  between operations  1.95 us (3%)
  other arithmetic  1.86 us (3%)
    pallas_call x1, Pallas kernels, per_device(): pl.pallas_call(kernel, out_shape=(rows, rows, jax.ShapeDtypeStruct((8, 12...  54.9 us

profile of v4, /device:TPU:1, one launch (start us, length us, event | category | flops | bytes accessed | tf_op | source)
XLA Modules:
  0.0 59.3 jit_solution(12741421890657191620)
XLA Ops:
  1.9 0.0 copy-start
  1.9 1.0 %pad_maximum_fusion.emb_ref = bf16[128,1152]{1,0:T(8,128)(2,1)S(1)} fusion(bf16[64,1152]{1,0:T(8,128)(2,1)} %bitcast.12, bf16[64,1152]{1,0:T(8,128)(2,1)} %param.5), kind=kLoop, calls=%fused_computation | loop fusion | flops 589824 | bytes 589824 | tf_op jit(solution)/shard_map/concatenate | solution.py:516
  2.9 0.0 copy-done
  3.0 54.9 %shard_map.92 = (f32[64,1152]{1,0:T(8,128)S(1)}, f32[64,1152]{1,0:T(8,128)S(1)}, f32[8,128]{1,0:T(8,128)S(1)}) custom-call(bf16[128,1152]{1,0:T(8,128)(2,1)S(1)} %pad_maximum_fusion.emb_ref, s32[8,128]{1,0:T(8,128)S(1)} %bitcast.10, f32[1,1]{1,0:T(1,128)} %bitcast.8.log_temp_ref, f32[1,1]{1,0:T(1,128)} %bitcast.9.bias_ref), custom_call_target="tpu_custom_call" | custom-call | flops 7247757312 | bytes 900000 | tf_op jit(solution)/shard_map/pallas_call | solution.py:477
  57.9 0.5 fusion
  58.4 0.8 %broadcast_multiply_fusion = (f32[64,1152]{1,0:T(8,128)}, f32[64,1152]{1,0:T(8,128)}) fusion(f32[64,1152]{1,0:T(8,128)S(1)} %get-tuple-element.12, f32[64,1152]{1,0:T(8,128)S(1)} %get-tuple-element.11), kind=kLoop, calls=%fused_computation.1 | loop fusion | flops 147456 | bytes 1179648 | tf_op jit(solution)/shard_map/mul | solution.py:517
Async XLA Ops:
  1.9 1.0 %copy-start = (s32[1024]{0:T(1024)S(1)}, s32[1024]{0:T(1024)}, u32[]{:S(2)}) copy-start(s32[1024]{0:T(1024)} %param.7) | copy-start | bytes 12292
